TPU v7x, 256 devices: a whole 4x4x8 slice. The times are simulated.
256 devices in a mesh: brick: 64 (over x, y_lo, z), row: 4 (over y_hi, core).
Axes of the slice: x: 4, y: 4 (y_hi: 2, y_lo: 2; y = y_hi * 2 + y_lo), z: 8, core: 2. Of those that a mesh axis runs over, the one named last changes fastest.
Arguments:
- magnet: float32 [3, 512, 128, 256], P(None, 'brick', 'row'), may hold values from -6 to 6
- node_position: float32 [3, 98304], replicated, may hold values from 0 to 8
- node_moment: float32 [3, 98304], replicated, may hold values from -5 to 5
- solid_fraction: float32 [98304], replicated, may hold values from 0.3 to 0.7
- request_cell: int32 [64, 4, 64, 12], P('brick', 'row'), may hold values from 0 to 65535, as said below
- request_slot: int32 [64, 4, 64, 12], P('brick', 'row'), may hold values from 0 to 1535, as said below
- request_count: int32 [64, 4, 64], P('brick', 'row'), may hold values from 0 to 12, as said below
Outputs:
- potential: float32 [512, 128, 256], P('brick', 'row')
- boundary_u2: float32 [64, 4, 64, 12], P('brick', 'row')
Inputs may be any that keep to these rules, and one draw needn't show every extreme that they name: `request_count`: over all devices, the counts toward one column block sum to 1536; some device's count is exactly 12 in every column block. `request_slot`: over all devices, the live slots toward column block b name each of its 1536 positions exactly once; dead slots hold arbitrary positions. `request_cell`: the live slots of one device name distinct cells.
All inputs are finite; a program needn't handle non-finite values.
Results may differ from a plain program's by a relative error of at most 0.0003.
Values sent between devices are 32-bit elements; how exact they have to be, the bound alone decides.
No kernel may reach another device: no remote copies, remote signals or barrier semaphores. Data moves between devices by JAX's collectives and lax.ppermute only.
A program may use at most 64 MiB of HBM per device.

v0:
```python
import math

import jax
import jax.numpy as jnp
from jax import lax
from jax.sharding import PartitionSpec as P

CX = 8
CY = 32
CZ = 256
NODES_DEV = 384
SWEEPS = 12


RELAX_LOW = 0.5
RELAX_HIGH = 2.0
SOFTENING = 0.5


def padded_2(x, sides, width):
    for axis, dim in sides:
        devices, length = (lax.axis_size(axis), x.shape[dim])
        up = [(i, (i + 1) % devices) for i in range(devices - 1)]
        down = [(j, i) for i, j in up]
        last = lax.slice_in_dim(x, length - width, length, axis=dim)
        first = lax.slice_in_dim(x, 0, width, axis=dim)
        before = lax.ppermute(last, axis, up)
        after = lax.ppermute(first, axis, down)
        x = jnp.concatenate([before, x, after], axis=dim)
    return x


def sweep_weights(total_steps):
    centre = 0.5 * (RELAX_HIGH + RELAX_LOW)
    radius = 0.5 * (RELAX_HIGH - RELAX_LOW)
    root_list = [
        1.0 / (centre + radius * math.cos(math.pi * (2 * order_index + 1) / (2 * total_steps)))
        for order_index in range(total_steps)
    ]
    ordered = []
    for order_index in range(total_steps // 2):
        ordered.append(root_list[order_index])
        ordered.append(root_list[total_steps - 1 - order_index])
    return ordered


def shift_depth(planes):
    zeros_plane = jnp.zeros(planes.shape[:2] + (1,), planes.dtype)
    upward = jnp.concatenate([planes[:, :, 1:], zeros_plane], axis=2)
    downward = jnp.concatenate([zeros_plane, planes[:, :, :-1]], axis=2)
    return (upward, downward)


def beside_sum(padded):
    centre = padded[1:-1, 1:-1]
    upward, downward = shift_depth(centre)
    neighbours = (
        padded[2:, 1:-1]
        + padded[:-2, 1:-1]
        + padded[1:-1, 2:]
        + padded[1:-1, :-2]
        + upward
        + downward
    )
    return (centre, neighbours)


def divergence(padded):
    along_x = padded[0, 2:, 1:-1] - padded[0, :-2, 1:-1]
    along_y = padded[1, 1:-1, 2:] - padded[1, 1:-1, :-2]
    upward, downward = shift_depth(padded[2, 1:-1, 1:-1])
    return -0.5 * (along_x + along_y + (upward - downward))


def relax(centre, neighbours, source, weight):
    return centre + weight * (source - 6.0 * centre + neighbours) / 6.0


def double_layer(targets, sources, moments):
    delta_x = targets[0][:, None] - sources[0][None, :]
    delta_y = targets[1][:, None] - sources[1][None, :]
    delta_z = targets[2][:, None] - sources[2][None, :]
    distance_sq = delta_x * delta_x + delta_y * delta_y + delta_z * delta_z + SOFTENING
    facing = (
        moments[0][None, :] * delta_x
        + moments[1][None, :] * delta_y
        + moments[2][None, :] * delta_z
    )
    return facing / (4.0 * math.pi * distance_sq * jnp.sqrt(distance_sq))


def local(
    magnet, node_position, node_moment, solid_fraction, request_cell, request_slot, request_count
):
    weights = sweep_weights(SWEEPS)
    weight_list = jnp.array(weights, jnp.float32)
    brick_count = lax.axis_size("brick")
    row_count = lax.axis_size("row")
    brick_index = lax.axis_index("brick")
    row_index = lax.axis_index("row")
    cap_slots = request_cell.shape[3]
    block_len = NODES_DEV * row_count
    cell_total = CX * CY * CZ
    own_cells = request_cell[0, 0]
    own_slots = request_slot[0, 0]
    live_slot = jnp.arange(cap_slots)[None, :] < request_count[0, 0][:, None]
    asked_slots = jnp.where(live_slot, own_slots, block_len)
    received_slots = lax.all_to_all(asked_slots, "brick", split_axis=0, concat_axis=0, tiled=True)
    all_slots = lax.all_gather(received_slots, "row", axis=0, tiled=True)
    grouped = node_position.reshape(3, brick_count, row_count, NODES_DEV)
    targets = lax.dynamic_index_in_dim(grouped, row_index, 2, keepdims=False).reshape(
        3, brick_count * NODES_DEV
    )
    sources = lax.dynamic_slice_in_dim(node_position, brick_index * block_len, block_len, 1)
    moments = lax.dynamic_slice_in_dim(node_moment, brick_index * block_len, block_len, 1)
    zero_field = jnp.zeros((CX, CY, CZ), jnp.float32)
    padded_magnet = padded_2(magnet, (("brick", 1), ("row", 2)), 1)
    source = divergence(padded_magnet)

    def single_sweep(sweep_index, current):
        padded = padded_2(current, (("brick", 0), ("row", 1)), 1)
        centre, neighbours = beside_sum(padded)
        return relax(centre, neighbours, source, weight_list[sweep_index])

    first_field = lax.fori_loop(0, SWEEPS, single_sweep, zero_field)
    picked = jnp.take(first_field.reshape(-1), own_cells.reshape(-1)).reshape(live_slot.shape)
    traces = jnp.where(live_slot, picked, 0.0)
    received_traces = lax.all_to_all(traces, "brick", split_axis=0, concat_axis=0, tiled=True)
    all_traces = lax.all_gather(received_traces, "row", axis=0, tiled=True)
    column_values = (
        jnp.zeros((block_len,), jnp.float32)
        .at[all_slots.reshape(-1)]
        .add(all_traces.reshape(-1), mode="drop")
    )
    tile_rows = targets.shape[1]
    piece_rows = math.gcd(tile_rows, 512)

    def joined_rows(row_start):
        piece = lax.dynamic_slice_in_dim(targets, row_start, piece_rows, 1)
        return jnp.dot(
            double_layer(piece, sources, moments), column_values, precision=lax.Precision.HIGHEST
        )

    row_starts = jnp.arange(tile_rows // piece_rows) * piece_rows
    partial_sums = lax.map(joined_rows, row_starts).reshape(-1)
    brick_range = jnp.arange(brick_count)
    node_ids = jnp.where(live_slot, brick_range[:, None] * block_len + own_slots, 0)
    row_values = lax.psum(partial_sums, "brick")
    every_node = lax.all_gather(row_values, "row", axis=0, tiled=True)
    every_node = (
        every_node.reshape(row_count, brick_count, NODES_DEV).transpose(1, 0, 2).reshape(-1)
    )
    returned = jnp.take(every_node, node_ids.reshape(-1)).reshape(live_slot.shape)
    fraction = jnp.take(solid_fraction, node_ids.reshape(-1)).reshape(live_slot.shape)
    boundary = jnp.where(live_slot, returned + (fraction - 1.0) * traces, 0.0)
    clamp_index = jnp.where(live_slot, own_cells, cell_total).reshape(-1)
    clamp_values = (
        jnp.zeros((cell_total,), jnp.float32)
        .at[clamp_index]
        .set(boundary.reshape(-1), mode="drop")
        .reshape(CX, CY, CZ)
    )
    clamp_mask = (
        jnp.zeros((cell_total,), jnp.bool_)
        .at[clamp_index]
        .set(True, mode="drop")
        .reshape(CX, CY, CZ)
    )
    start_field = jnp.where(clamp_mask, clamp_values, 0.0)

    def second_sweep(sweep_index, current):
        padded = padded_2(current, (("brick", 0), ("row", 1)), 1)
        centre, neighbours = beside_sum(padded)
        return jnp.where(
            clamp_mask, clamp_values, relax(centre, neighbours, 0.0, weight_list[sweep_index])
        )

    second_field = lax.fori_loop(0, SWEEPS, second_sweep, start_field)
    return (first_field + second_field, boundary[None, None])


def solution(mesh):
    placed = (
        P(None, "brick", "row", None),
        P(),
        P(),
        P(),
        P("brick", "row", None, None),
        P("brick", "row", None, None),
        P("brick", "row", None),
    )
    return jax.shard_map(
        local,
        mesh=mesh,
        in_specs=placed,
        out_specs=(P("brick", "row", None), P("brick", "row", None, None)),
        check_vma=False,
    )
```

profile of v0, /device:TPU:1, one launch (start us, length us, event | category | flops | bytes accessed | tf_op | source)
XLA Modules:
  0.0 1530.0 jit_solution(15773466756482924096)
XLA Ops:
  16.7 14.3 all-to-all-start
  46.9 5.8 all-gather
  55.7 215.4 %while.41 = (s32[]{:T(128)}, f32[8,32,256]{2,1,0:T(8,128)S(1)}, f32[8,32,256]{2,1,0:T(8,128)S(1)}, s32[]{:T(128)}, s32[]{:T(128)}, /*index=5*/f32[12]{0:T(128)S(1)}) while((s32[]{:T(128)}, f32[8,32,256]{2,1,0:T(8,128)S(1)}, f32[8,32,256]{2,1,0:T(8,128)S(1)}, s32[]{:T(128)}, s32[]{:T(128)}, ...), condition=%wide.region_1.2_spmd.clone.clone, body=%wide.region_0.1_spmd.sunk.clone.clone.sunk | while | flops 1320963 | bytes 3787007 | solution.py:125
  162.6 5.8 collective-permute-start.5
  180.9 5.8 collective-permute-start.5
  199.2 5.8 collective-permute-start.5
  217.5 5.8 collective-permute-start.5
  235.8 5.8 collective-permute-start.5
  254.1 5.8 collective-permute-start.5
  276.5 36.8 %all-to-all-start.1 = ((f32[64,1,12]{2,1,0:T(1,128)}), f32[64,1,12]{2,1,0:T(1,128)S(1)}, u32[]{:S(2)}, u32[]{:S(2)}) async-start(f32[64,1,12]{2,1,0:T(1,128)} %bitcast.12), calls=%async_computation.1 | async-start | bytes 65536 | tf_op jit(solution)/shard_map/all_to_all | solution.py:128
  313.4 9.1 all-to-all-done.1
  322.5 5.8 all-gather.1
  329.8 18.8 %scatter_custom_fusion.1 = f32[1536]{0:T(1024)S(1)} fusion(s32[3072]{0:T(1024)S(1)} %bitcast.72, f32[3072]{0:T(1024)S(1)} %reshape.400, f32[]{:T(128)} %constant.145.clone.1), kind=kCustom, calls=%fused_computation.114 | custom fusion | flops 3072 | bytes 6148 | tf_op jit(solution)/shard_map/scatter-add | solution.py:133
  349.3 409.9 %while.42 = (s32[]{:T(128)}, f32[48,512]{1,0:T(8,128)S(1)}, f32[3,1536]{1,0:T(4,128)S(1)}, s32[48]{0:T(128)S(1)}, f32[3,24576]{1,0:T(4,128)S(1)}, /*index=5*/f32...) while((s32[]{:T(128)}, f32[48,512]{1,0:T(8,128)S(1)}, ...), condition=%wide.wide.region_5.6_spmd, body=%wide.wide.region_4.5_spmd.sunk | while | flops 22806536 | bytes 141523 | solution.py:145
  352.0 5.7 fusion.85
  360.6 5.7 fusion.85
  369.1 5.7 fusion.85
  377.6 5.7 fusion.85
  386.2 5.7 fusion.85
  394.7 5.7 fusion.85
  403.3 5.7 fusion.85
  411.8 5.7 fusion.85
  420.3 5.7 fusion.85
  428.9 5.7 fusion.85
  437.4 5.7 fusion.85
  446.0 5.7 fusion.85
  454.5 5.7 fusion.85
  463.0 5.7 fusion.85
  768.1 484.0 %all-reduce.8.cloned.1.call-done = f32[24576]{0:T(1024)} async-done(((f32[24576]{0:T(1024)}), f32[24576]{0:T(1024)}) %all-reduce.8.cloned.1.call-update) | async-done | bytes 98320 | tf_op jit(solution)/shard_map/psum | solution.py:148
  1252.2 33.8 %all_gather.11 = f32[98304]{0:T(1024)S(1)} all-gather(f32[24576]{0:T(1024)} %all-reduce.8.cloned.1.call-done), channel_id=1, replica_groups=mesh['brick'=64,'row'=4] {'row'}, dimensions={0}, use_global_device_ids=true | all-gather | bytes 491520 | tf_op jit(solution)/shard_map/all_gather | solution.py:149
  1295.5 226.8 %while.40 = (s32[]{:T(128)}, f32[8,32,256]{2,1,0:T(8,128)S(1)}, pred[8,32,256]{2,1,0:T(8,128)(4,1)S(1)}, f32[8,32,256]{2,1,0:T(8,128)S(1)}, s32[]{:T(128)}, /*index=5*/f32[12]{0:T(128)S(1)}) while((s32[]{:T(128)}, f32[8,32,256]{2,1,0:T(8,128)S(1)}, pred[8,32,256]{2,1,0:T(8,128)(4,1)S(1)}, f32[8,32,256]{2,1,0:T(8,128)S(1)}, ...), condition=%wide.region_9.11_spmd.clone, body=%wide.region_8.10_spmd.sunk.clone.sunk | while | flops 1048578 | bytes 4528373 | solution.py:178
  1303.9 5.8 collective-permute-start.2
  (682 shorter events, 688.9 us)
Async XLA Ops:
  8.9 29.1 %collective-permute-start.9 = (f32[3,1,32,256]{3,2,1,0:T(8,128)}, f32[3,1,32,256]{3,2,1,0:T(8,128)S(1)}, u32[]{:S(2)}, u32[]{:S(2)}) collective-permute-start(f32[3,1,32,256]{3,2,1,0:T(8,128)} %get-tuple-element.325), channel_id=1, source_target_pairs={{0,4},{4,8},{8,12},{12,16},{16,20},{20,24},{24,28},{28,32},{32,36}... | collective-permute-start | bytes 294920 | tf_op jit(solution)/shard_map/ppermute | solution.py:27
  13.2 24.8 %collective-permute-start.8 = (f32[3,1,32,256]{3,2,1,0:T(8,128)}, f32[3,1,32,256]{3,2,1,0:T(8,128)S(1)}, u32[]{:S(2)}, u32[]{:S(2)}) collective-permute-start(f32[3,1,32,256]{3,2,1,0:T(8,128)} %get-tuple-element.324), channel_id=1, source_target_pairs={{4,0},{8,4},{12,8},{16,12},{20,16},{24,20},{28,24},{32,28},{36,32}... | collective-permute-start | bytes 294920 | tf_op jit(solution)/shard_map/ppermute | solution.py:28
  16.7 30.2 %all-to-all-start = ((s32[64,1,12]{2,1,0:T(1,128)}), s32[64,1,12]{2,1,0:T(1,128)S(1)}, u32[]{:S(2)}, u32[]{:S(2)}) async-start(s32[64,1,12]{2,1,0:T(1,128)} %bitcast.9), calls=%async_computation | async-start | bytes 65536 | tf_op jit(solution)/shard_map/all_to_all | solution.py:108
  38.8 15.7 %collective-permute-start.10 = (f32[3,10,1,256]{3,2,1,0:T(1,128)}, f32[3,10,1,256]{3,2,1,0:T(1,128)}, u32[]{:S(2)}, u32[]{:S(2)}) collective-permute-start(f32[3,10,1,256]{3,2,1,0:T(1,128)} %get-tuple-element.322), channel_id=1, source_target_pairs={{1,0},{2,1},{3,2},{5,4},{6,5},{7,6},{9,8},{10,9},{11,10},{13,12},{... | collective-permute-start | bytes 92168 | tf_op jit(solution)/shard_map/ppermute | solution.py:28
  42.2 12.3 collective-permute-start.11
  62.0 7.9 collective-permute-start.6
  67.3 6.5 collective-permute-start.7
  101.5 6.7 collective-permute-start.7
  135.7 6.7 collective-permute-start.7
  143.3 6.8 collective-permute-start.4
  144.6 6.6 collective-permute-start.5
  153.9 6.5 collective-permute-start.7
  161.3 7.1 collective-permute-start.4
  162.6 6.8 collective-permute-start.5
  172.2 6.5 collective-permute-start.7
  179.6 7.1 collective-permute-start.4
  180.9 6.8 collective-permute-start.5
  197.9 7.1 collective-permute-start.4
  199.2 6.8 collective-permute-start.5
  208.8 6.5 collective-permute-start.7
  216.2 7.1 collective-permute-start.4
  217.5 6.8 collective-permute-start.5
  227.1 6.5 collective-permute-start.7
  234.5 7.1 collective-permute-start.4
  235.8 6.8 collective-permute-start.5
  245.4 6.5 collective-permute-start.7
  252.8 7.1 collective-permute-start.4
  254.1 6.8 collective-permute-start.5
  276.5 46.0 %all-to-all-start.1 = ((f32[64,1,12]{2,1,0:T(1,128)}), f32[64,1,12]{2,1,0:T(1,128)S(1)}, u32[]{:S(2)}, u32[]{:S(2)}) async-start(f32[64,1,12]{2,1,0:T(1,128)} %bitcast.12), calls=%async_computation.1 | async-start | bytes 65536 | tf_op jit(solution)/shard_map/all_to_all | solution.py:128
  313.3 938.9 %all-reduce.8.cloned.1.call-start = ((), (), s32[]{:S(2)}) async-start(), calls=%async_computation.2 | async-start | bytes 196608 | tf_op jit(solution)/shard_map/psum | solution.py:148
  1303.9 8.5 collective-permute-start.2
  1309.7 6.5 collective-permute-start.3
  (80 other events, 1280.1 us)
Sparse Core Ops, SparseCore 0:
  760.0 492.0 all-reduce.7
where the time goes:
time: 1540 us; the launch traced here: 1530 us
  waiting for transfers between devices  639 us (41%)
  starting transfers between devices  320 us (21%)
  matrix products  276 us (18%)
  loops' own time  97.1 us (6%)
  local copies, waits for them, and re-layouts  91.8 us (6%)
  other arithmetic  46.2 us (3%)
  blocking collectives  45.3 us (3%)
    psum x1, waiting for transfers between devices, local(): row_values = lax.psum(partial_sums, 'brick')  484 us
    dot_general x48, matrix products, joined_rows(): jnp.dot(double_layer(piece, sources, moments), column_values, precision=l...  276 us
    ppermute x50, starting transfers between devices, padded_2(): before = lax.ppermute(last, axis, up)  187 us
    ppermute x50, waiting for transfers between devices, padded_2(): after = lax.ppermute(first, axis, down)  134 us
    another operation x1, loops' own time, local(): partial_sums = lax.map(joined_rows, row_starts).reshape(-1)  94.8 us
    ppermute x50, starting transfers between devices, padded_2(): after = lax.ppermute(first, axis, down)  81.8 us
    all_to_all x1, starting transfers between devices, local(): lax.all_to_all(traces, 'brick', split_axis=0, concat_axis=0, tiled=True)  36.8 us
    all_gather x1, blocking collectives, local(): every_node = lax.all_gather(row_values, 'row', axis=0, tiled=True)  33.8 us
  transfers between devices with their start and end apart: 103, of which 50 were waited for; matrix products, arithmetic and copies ran while one was open for 2% of the time, Pallas kernels for 0%

commit v1 on v0

v1 whole, which is shorter than its diff:
```python
import functools
import math

import jax
import jax.numpy as jnp
from jax import lax
from jax.experimental import pallas as pl
from jax.experimental.pallas import tpu as pltpu
from jax.sharding import PartitionSpec as P

CX = 8
CY = 32
CZ = 256
SWEEPS = 12
CAP = 12
RELAX_LOW = 0.5
RELAX_HIGH = 2.0
SOFTENING = 0.5

YO = 12
YE = CY + 24
XS = CX + 22
XD = CX + 24
HALF = 128
PARAMS = pltpu.CompilerParams(vmem_limit_bytes=50 * 1024 * 1024)
DEAD_SLOT = 4096
TINY = 1e-30
F32 = jnp.float32
BF16 = jnp.bfloat16
VMEM = pl.BlockSpec(memory_space=pltpu.VMEM)
SMEM = pl.BlockSpec(memory_space=pltpu.SMEM)


def sweep_weights(total_steps):
    centre = 0.5 * (RELAX_HIGH + RELAX_LOW)
    radius = 0.5 * (RELAX_HIGH - RELAX_LOW)
    root_list = [
        1.0 / (centre + radius * math.cos(math.pi * (2 * order_index + 1) / (2 * total_steps)))
        for order_index in range(total_steps)
    ]
    ordered = []
    for order_index in range(total_steps // 2):
        ordered.append(root_list[order_index])
        ordered.append(root_list[total_steps - 1 - order_index])
    return ordered


WEIGHTS = sweep_weights(SWEEPS)


def shaped(*dims, dtype=F32):
    return jax.ShapeDtypeStruct(dims, dtype)


def split3(v):
    hi = v.astype(BF16).astype(F32)
    rest = v - hi
    mid = rest.astype(BF16).astype(F32)
    return hi, mid, rest - mid


def z_pair(left, right):
    lane = lax.broadcasted_iota(jnp.int32, left.shape, 1)
    left_dn = pltpu.roll(left, 1, 1)
    right_dn = pltpu.roll(right, 1, 1)
    left_up = pltpu.roll(left, HALF - 1, 1)
    right_up = pltpu.roll(right, HALF - 1, 1)
    first, last = lane == 0, lane == HALF - 1
    dn = (jnp.where(first, 0.0, left_dn), jnp.where(first, left_dn, right_dn))
    up = (jnp.where(last, right_up, left_up), jnp.where(last, 0.0, right_up))
    return dn, up


def source_kernel(m_ref, e_ref, low_ref, high_ref, pad):
    pad[...] = jnp.zeros_like(pad)
    for x in range(CX):
        pad[0, x + 1, 12:44, :] = m_ref[0, x]
        pad[1, x + 1, 12:44, :] = m_ref[1, x]
        pad[2, x + 1, 12:44, :] = m_ref[2, x]
    zeros = jnp.zeros((40, CZ), F32)
    for i in range(CX + 2):
        ahead = pad[0, i + 1, 8:48, :] if i + 1 <= CX else zeros
        behind = pad[0, i - 1, 8:48, :] if i >= 2 else zeros
        total = ahead - behind
        if 1 <= i <= CX:
            total = total + (pad[1, i, 9:49, :] - pad[1, i, 7:47, :])
            c = pad[2, i, 8:48, :]
            dn, up = z_pair(c[:, :HALF], c[:, HALF:])
            total = total + jnp.concatenate([up[0] - dn[0], up[1] - dn[1]], axis=1)
        total = -0.5 * total
        e_ref[i] = total
        if i < 4:
            low_ref[i] = total
        if i >= CX - 2:
            high_ref[i - (CX - 2)] = total


def own_source(magnet):
    return pl.pallas_call(
        source_kernel,
        out_shape=(shaped(10, 40, CZ), shaped(4, 40, CZ), shaped(4, 40, CZ)),
        in_specs=[VMEM],
        out_specs=(VMEM, VMEM, VMEM),
        scratch_shapes=[pltpu.VMEM((3, CX + 2, 56, CZ), F32)],
        compiler_params=PARAMS,
        name="own_source",
    )(magnet)


def join_kernel(e_ref, l1_ref, r1_ref, l2_ref, r2_ref, sx_ref, upper_ref, lower_ref):
    parts = ((e_ref, 10, 10), (l1_ref, 2, 10), (r1_ref, 18, 10), (l2_ref, 0, 4), (r2_ref, 26, 4))
    for plane in range(XS):
        total = None
        for ref, begin, count in parts:
            if begin <= plane < begin + count:
                term = ref[plane - begin]
                total = term if total is None else total + term
        sx_ref[plane] = total
        upper_ref[plane] = total[24:40]
        lower_ref[plane] = total[0:16]


def join_x(own, l1, r1, l2, r2):
    return pl.pallas_call(
        join_kernel,
        out_shape=(shaped(XS, 40, CZ), shaped(XS, 16, CZ), shaped(XS, 16, CZ)),
        in_specs=[VMEM] * 5,
        out_specs=(VMEM,) * 3,
        compiler_params=PARAMS,
        name="join_x",
    )(own, l1, r1, l2, r2)


def neighbours(src, x):
    c = src[x]
    around_x = src[x - 1] + src[x + 1]
    halves = (c[:, :HALF], c[:, HALF:])
    dn, up = z_pair(*halves)
    out = []
    for h in range(2):
        v = halves[h]
        around_y = pltpu.roll(v, 1, 0) + pltpu.roll(v, YE - 1, 0)
        around = around_x[:, h * HALF : (h + 1) * HALF] + around_y + (dn[h] + up[h])
        out.append((v, around))
    return out


def first_kernel(place_ref, sx_ref, below_ref, above_ref, cell_ref, base_ref, field_ref, msg_ref, s, buf):
    brick, row = place_ref[0], place_ref[1]
    cells_x, cells_y = place_ref[2], place_ref[3]
    y_at = lax.broadcasted_iota(jnp.int32, (YE, HALF), 0) + (row * CY - YO)
    in_y = jnp.where((y_at >= 0) & (y_at < cells_y), 1.0, 0.0).astype(F32)

    def x_scale(x, scale):
        at = brick * CX + x - 11
        return jnp.where((at >= 0) & (at < cells_x), scale, 0.0).astype(F32)

    def gather_plane(x, carry):
        t = sx_ref[x]
        lo = below_ref[x]
        hi = above_ref[x]
        full = jnp.concatenate(
            [lo[0:8], t[0:8] + lo[8:16], t[8:32], t[32:40] + hi[0:8], hi[8:16]], axis=0
        )
        s[x] = full
        coef = in_y * x_scale(x, WEIGHTS[0] / 6.0)
        buf[0, x, :, :HALF] = coef * full[:, :HALF]
        buf[0, x, :, HALF:] = coef * full[:, HALF:]
        return carry

    lax.fori_loop(0, XS, gather_plane, 0)
    for k in range(1, SWEEPS):
        weight = WEIGHTS[k]
        src, dst = buf.at[(k - 1) % 2], buf.at[k % 2]

        def plane(x, carry, src=src, dst=dst, weight=weight):
            coef = in_y * x_scale(x, weight / 6.0)
            source = s[x]
            for h, (v, around) in enumerate(neighbours(src, x)):
                lanes = slice(h * HALF, (h + 1) * HALF)
                dst[x, :, lanes] = (1.0 - weight) * v + coef * (source[:, lanes] + around)
            return carry

        lax.fori_loop(k, XS - k, plane, 0)
    last = (SWEEPS - 1) % 2
    for x in range(CX):
        field_ref[x] = buf[last, x + 11, YO : YO + CY, :]
    flat = field_ref[...].reshape(CX * CY, CZ)
    turned = flat.T
    parts = [p.astype(BF16) for p in split3(turned)]
    row_at = lax.broadcasted_iota(jnp.int32, (CX * CY, HALF), 0)
    picked = []
    for k in range(6):
        cell = cell_ref[k : k + 1, :]
        hot = jnp.where(row_at == (cell >> 8), 1.0, 0.0).astype(BF16)
        at_rows = sum(jnp.dot(p, hot, preferred_element_type=F32) for p in parts)
        kept = jnp.where(row_at == (cell & 255), at_rows, 0.0)
        picked.append(jnp.sum(kept, axis=0, keepdims=True))
    sub = lax.broadcasted_iota(jnp.int32, (HALF, HALF), 0)
    tile = jnp.zeros((HALF, HALF), F32)
    for k in range(6):
        tile = jnp.where(sub == k, picked[k], tile)
    turned_tile = tile.T
    both = turned_tile[0:64] + pltpu.roll(turned_tile[64:128], 6, 1)
    traces = pltpu.roll(both, CAP, 1)
    lanes = 3 * CAP
    full = base_ref[...] + traces[:, :lanes]
    for q in range(4):
        msg_ref[q] = full


def first_solve(place, sx, below, above, cells, base):
    return pl.pallas_call(
        first_kernel,
        out_shape=(shaped(CX, CY, CZ), shaped(4, 64, 3 * CAP)),
        in_specs=[SMEM] + [VMEM] * 5,
        out_specs=(VMEM, VMEM),
        scratch_shapes=[pltpu.VMEM((XS, YE, CZ), F32), pltpu.VMEM((2, XS, YE, CZ), F32)],
        compiler_params=PARAMS,
        name="first_solve",
    )(place, sx, below, above, cells, base)


def place_kernel(place_ref, got_ref, out_ref):
    row = place_ref[1]
    got = got_ref[...]
    at = (lax.broadcasted_iota(jnp.int32, (256, 384), 1) + row * 384).astype(F32)
    acc = jnp.zeros((256, 384), F32)
    for i in range(CAP):
        slot = got[:, i : i + 1]
        trace = got[:, CAP + i : CAP + i + 1]
        acc = acc + jnp.where(at == slot, trace, 0.0)
    total = jnp.sum(acc, axis=0, keepdims=True)
    out_ref[...] = jnp.broadcast_to(total, (64, 384))


def place_quarter(place, got):
    return pl.pallas_call(
        place_kernel,
        out_shape=shaped(64, 384),
        in_specs=[SMEM, VMEM],
        out_specs=VMEM,
        compiler_params=PARAMS,
        name="place_quarter",
    )(place, got)


SRC = 24576
CHUNK = 768
TILE = 128


def stack_six(v, order):
    parts = split3(v)
    return jnp.concatenate([parts[i] for i in order], axis=0)


RIGHT = (0, 1, 2, 0, 1, 0)
LEFT = (0, 0, 0, 1, 1, 2)


def prepare_kernel(target_ref, source_ref, left_ref, right_ref, moment_ref):
    sub = lax.broadcasted_iota(jnp.int32, (8, CHUNK), 0)

    def sources(c, carry):
        at = pl.multiple_of(c * CHUNK, CHUNK)
        v = source_ref[:, pl.ds(at, CHUNK)]
        pos = v[0:3] - 4.0
        mom = v[3:6]
        norm = jnp.sum(pos * pos, axis=0, keepdims=True)
        across = jnp.sum(pos * mom, axis=0, keepdims=True)
        dist = jnp.where(sub == 3, 1.0, jnp.where(sub == 4, norm, 0.0))
        face = jnp.where(sub == 4, -across, 0.0)
        for i in range(3):
            dist = jnp.where(sub == i, -2.0 * pos[i : i + 1], dist)
            face = jnp.where(sub == i, mom[i : i + 1], face)
        right_ref[:, pl.ds(at, CHUNK)] = stack_six(dist, RIGHT).astype(BF16)
        moment_ref[:, pl.ds(at, CHUNK)] = face
        return carry

    lax.fori_loop(0, SRC // CHUNK, sources, 0)
    sub = lax.broadcasted_iota(jnp.int32, (8, TILE), 0)
    for t in range(1536 // TILE):
        pos = target_ref[0:3, t * TILE : (t + 1) * TILE] - 4.0
        norm = jnp.sum(pos * pos, axis=0, keepdims=True) + SOFTENING
        feat = jnp.where(sub == 3, norm, jnp.where(sub == 4, 1.0, 0.0))
        for i in range(3):
            feat = jnp.where(sub == i, pos[i : i + 1], feat)
        rows = jnp.concatenate([stack_six(feat, LEFT), jnp.zeros((HALF - 48, TILE), F32)], axis=0)
        left_ref[t * TILE : (t + 1) * TILE, :] = rows.T[:, :48].astype(BF16)


def prepare(targets, sources):
    return pl.pallas_call(
        prepare_kernel,
        out_shape=(shaped(1536, 48, dtype=BF16), shaped(48, SRC, dtype=BF16), shaped(8, SRC)),
        in_specs=[VMEM, VMEM],
        out_specs=(VMEM, VMEM, VMEM),
        compiler_params=PARAMS,
        name="prepare",
    )(targets, sources)


def layer_kernel(place_ref, left_ref, right_ref, moment_ref, trace_ref, fraction_ref, out_ref, acc):
    brick, row = place_ref[0], place_ref[1]
    acc[...] = jnp.zeros_like(acc)

    def chunk(c, carry):
        at = pl.multiple_of(c * CHUNK, CHUNK)
        trace = jnp.concatenate(
            [trace_ref[pl.ds(2 * c, 1), :], trace_ref[pl.ds(2 * c + 1, 1), :]], axis=1
        )
        face = moment_ref[:, pl.ds(at, CHUNK)] * trace
        face = stack_six(face, RIGHT).astype(BF16)
        dist = right_ref[:, pl.ds(at, CHUNK)]
        for t in range(1536 // TILE):
            rows = slice(t * TILE, (t + 1) * TILE)
            left = left_ref[rows, :]
            total = acc[rows, :]
            for n in range(CHUNK // 256):
                lanes = slice(n * 256, (n + 1) * 256)
                d = jnp.dot(left, dist[:, lanes], preferred_element_type=F32)
                f = jnp.dot(left, face[:, lanes], preferred_element_type=F32)
                r = lax.rsqrt(d)
                term = (f * r) * (r * r)
                total = total + term[:, :HALF] + term[:, HALF:]
            acc[rows, :] = total
        return carry

    lax.fori_loop(0, SRC // CHUNK, chunk, 0)
    for t in range(1536 // TILE):
        turned = acc[t * TILE : (t + 1) * TILE, :].T
        total = jnp.sum(turned, axis=0, keepdims=True)
        out_ref[:, t * TILE : (t + 1) * TILE] = total * (1.0 / (4.0 * math.pi))
    at = pl.multiple_of(row * 384, 128)
    own = (fraction_ref[...] - 1.0) * trace_ref[pl.ds(brick, 1), :]
    out_ref[:, pl.ds(at, 384)] = out_ref[:, pl.ds(at, 384)] + own


def layer(place, left, right, moment, traces, fraction):
    return pl.pallas_call(
        layer_kernel,
        out_shape=shaped(1, 1536),
        in_specs=[SMEM] + [VMEM] * 5,
        out_specs=VMEM,
        scratch_shapes=[pltpu.VMEM((1536, HALF), F32)],
        compiler_params=PARAMS,
        name="layer",
    )(place, left, right, moment, traces, fraction)


def answer_kernel(place_ref, part_ref, got_ref, out_ref, wide, table):
    row = place_ref[1]
    total = jnp.sum(part_ref[...], axis=0, keepdims=True)
    wide[...] = jnp.zeros_like(wide)
    lane = lax.broadcasted_iota(jnp.int32, (256, HALF), 1)
    wide[:, 0 : 3 * CAP] = got_ref[...]
    got = wide[...]
    slot = got.astype(jnp.int32)
    upper, lower = slot >> 7, slot & 127
    value = jnp.zeros((256, HALF), F32)
    for h in range(1536 // HALF):
        entry = jnp.broadcast_to(total[:, h * HALF : (h + 1) * HALF], (256, HALF))
        found = jnp.take_along_axis(entry, lower, axis=1)
        value = jnp.where(upper == h, found, value)
    cell = pltpu.roll(got, HALF - CAP, 1)
    pair = jnp.where(lane < CAP, value, jnp.where(lane < 2 * CAP, cell, 0.0))
    lane80 = lax.broadcasted_iota(jnp.int32, (80, HALF), 1)
    dead = jnp.where((lane80 >= CAP) & (lane80 < 2 * CAP), -1.0, 0.0)
    for q in range(6):
        table[q] = dead
    for q in range(4):
        table[q + 1, 8:72, :] = pair[q * 64 : (q + 1) * 64]
    for t in range(3):
        acc = jnp.zeros((64, HALF), F32)
        for s in range(5):
            piece = table[row + t, 6 + s : 70 + s, :]
            if s > 0:
                piece = pltpu.roll(piece, 2 * CAP * s, 1)
            acc = acc + piece
        out_ref[:, t * HALF : (t + 1) * HALF] = acc


def answer(place, partial, got):
    return pl.pallas_call(
        answer_kernel,
        out_shape=shaped(64, 384),
        in_specs=[SMEM, VMEM, VMEM],
        out_specs=VMEM,
        scratch_shapes=[pltpu.VMEM((256, HALF), F32), pltpu.VMEM((6, 80, HALF), F32)],
        compiler_params=PARAMS,
        name="answer",
    )(place, partial, got)


def second_kernel(place_ref, got_ref, first_ref, out_ref, mask, buf):
    brick, row = place_ref[0], place_ref[1]
    cells_x, cells_y = place_ref[2], place_ref[3]
    buf[0] = jnp.zeros((XD, YE, CZ), F32)
    z_at = lax.broadcasted_iota(jnp.int32, (CZ, HALF), 0)
    for t in range(3):
        block = got_ref[:, t * HALF : (t + 1) * HALF]
        turned = jnp.concatenate([block, pltpu.roll(block, HALF - 6, 1)], axis=0).T
        rows, begin = ((16, 0), (40, 8), (16, 40))[t]
        for s in range(5):
            planes, first_plane = ((4, 0), (8, 4), (8, 12), (8, 20), (4, 28))[s]
            x_off = 4 if s == 0 else 0
            hots, highs, lows = [], [], []
            row_at = lax.broadcasted_iota(jnp.int32, (planes * rows, HALF), 0)
            for k in range(6):
                value = turned[24 * s + k : 24 * s + k + 1, :]
                cell = turned[24 * s + CAP + k : 24 * s + CAP + k + 1, :].astype(jnp.int32)
                x = (cell >> 13) - x_off
                y = (cell >> 8) & 31
                live = (cell >= 0) & (x >= 0) & (x < planes)
                if t == 0:
                    live = live & (y >= 20)
                    y = y - 20
                else:
                    y = y + 4
                    if t == 2:
                        live = live & (y < 16)
                at = jnp.where(live, x * rows + y, -1)
                value = jnp.where(jnp.abs(value) < TINY, TINY, value)
                high = value.astype(BF16).astype(F32)
                hit = z_at == (cell & 255)
                hots.append(jnp.where(row_at == at, 1.0, 0.0).astype(BF16))
                highs.append(jnp.where(hit, high, 0.0).astype(BF16))
                lows.append(jnp.where(hit, value - high, 0.0).astype(BF16))
            hot = jnp.concatenate(hots, axis=1)
            total = None
            for part in (highs, lows):
                term = lax.dot_general(
                    hot, jnp.concatenate(part, axis=1), (((1,), (1,)), ((), ())), preferred_element_type=F32
                )
                total = term if total is None else total + term
            target = buf.at[0, first_plane : first_plane + planes, begin : begin + rows, :]
            target[...] = target[...] + total.reshape(planes, rows, CZ)
    y_at = lax.broadcasted_iota(jnp.int32, (YE, CZ), 0) + (row * CY - YO)
    in_y = (y_at >= 0) & (y_at < cells_y)

    def begin_plane(x, carry):
        v = buf[0, x]
        at = brick * CX + x - YO
        in_x = jnp.where((at >= 0) & (at < cells_x), 1.0, 0.0).astype(F32)
        mask[x] = jnp.where(in_y & (v == 0.0), in_x, 0.0)
        buf[0, x] = jnp.where(jnp.abs(v) < 2.0 * TINY, 0.0, v)
        return carry

    lax.fori_loop(0, XD, begin_plane, 0)
    for k in range(1, SWEEPS + 1):
        weight = WEIGHTS[k - 1]
        src, dst = buf.at[(k - 1) % 2], buf.at[k % 2]

        def plane(x, carry, src=src, dst=dst, weight=weight):
            free = mask[x]
            for h, (v, around) in enumerate(neighbours(src, x)):
                lanes = slice(h * HALF, (h + 1) * HALF)
                dst[x, :, lanes] = v + free[:, lanes] * ((weight / 6.0) * around - weight * v)
            return carry

        lax.fori_loop(k, XD - k, plane, 0)
    for x in range(CX):
        out_ref[x] = first_ref[x] + buf[SWEEPS % 2, x + YO, YO : YO + CY, :]


def second_solve(place, got, first):
    return pl.pallas_call(
        second_kernel,
        out_shape=shaped(CX, CY, CZ),
        in_specs=[SMEM, VMEM, VMEM],
        out_specs=VMEM,
        scratch_shapes=[pltpu.VMEM((XD, YE, CZ), F32), pltpu.VMEM((2, XD, YE, CZ), F32)],
        compiler_params=PARAMS,
        name="second_solve",
    )(place, got, first)


def shifted(x, axis, step):
    count = lax.axis_size(axis)
    pairs = [(i, i + step) for i in range(count) if 0 <= i + step < count]
    return lax.ppermute(x, axis, pairs)


def local(
    magnet, node_position, node_moment, solid_fraction, request_cell, request_slot, request_count
):
    bricks, rows = lax.axis_size("brick"), lax.axis_size("row")
    brick, row = lax.axis_index("brick"), lax.axis_index("row")
    place = jnp.stack([brick, row, jnp.int32(bricks * CX), jnp.int32(rows * CY)]).astype(jnp.int32)
    cell, slot = request_cell[0, 0], request_slot[0, 0]
    live = jnp.arange(CAP)[None, :] < request_count[0, 0][:, None]
    zeros = jnp.zeros((bricks, CAP), F32)
    slot_f = jnp.where(live, slot, DEAD_SLOT).astype(F32)
    cell_f = jnp.where(live, cell, -1).astype(F32)
    base = jnp.concatenate([slot_f, zeros, cell_f], axis=1)
    cells = cell.T.reshape(2, 6, bricks).transpose(1, 0, 2).reshape(6, 2 * bricks)
    grouped = jnp.concatenate([node_position, node_moment], axis=0).reshape(6, bricks, rows, 384)
    sources = lax.dynamic_index_in_dim(grouped, row, 2, keepdims=False).reshape(6, bricks * 384)
    targets = lax.dynamic_slice_in_dim(node_position, brick * 1536, 1536, 1)
    fraction = lax.dynamic_slice_in_dim(solid_fraction, brick * 1536 + row * 384, 384, 0)[None]
    left, right, moment = prepare(targets, sources)

    own, low, high = own_source(magnet)
    l1, r1 = shifted(own, "brick", 1), shifted(own, "brick", -1)
    l2, r2 = shifted(high, "brick", 2), shifted(low, "brick", -2)
    sx, upper, lower = join_x(own, l1, r1, l2, r2)
    below, above = shifted(upper, "row", 1), shifted(lower, "row", -1)
    first, message = first_solve(place, sx, below, above, cells, base)
    message = message.reshape(rows * bricks, 3 * CAP)
    got = lax.all_to_all(message, ("row", "brick"), split_axis=0, concat_axis=0, tiled=True)
    quarter = place_quarter(place, got)
    traces = lax.all_to_all(quarter, "brick", split_axis=0, concat_axis=0, tiled=True)
    partial = layer(place, left, right, moment, traces, fraction)
    partials = lax.all_gather(partial, "row", axis=0, tiled=True)
    reply = answer(place, partials, got)
    returned = lax.all_to_all(reply, "brick", split_axis=0, concat_axis=0, tiled=True)
    potential = second_solve(place, returned, first)
    begin = HALF + 2 * 2 * CAP
    boundary = jnp.where(live, returned[:, begin : begin + CAP], 0.0)
    return potential, boundary[None, None]


def solution(mesh):
    placed = (
        P(None, "brick", "row", None),
        P(),
        P(),
        P(),
        P("brick", "row", None, None),
        P("brick", "row", None, None),
        P("brick", "row", None),
    )
    return jax.shard_map(
        local,
        mesh=mesh,
        in_specs=placed,
        out_specs=(P("brick", "row", None), P("brick", "row", None, None)),
        check_vma=False,
    )
```

time: 1540 us -> 219 us (0.14)
  waiting for transfers between devices: 639 us -> 26.3 us
  starting transfers between devices: 320 us -> 41.9 us
  matrix products: 276 us -> 0 us
  Pallas kernels: 0 us -> 108 us
  loops' own time: 97.1 us -> 0 us
  local copies, waits for them, and re-layouts: 91.8 us -> 13.8 us
  other arithmetic: 46.2 us -> 3.99 us
  blocking collectives: 45.3 us -> 22.6 us
    psum x1 -> x0, waiting for transfers between devices: 484 us -> none  [local(): row_values = lax.psum(partial_sums, 'brick')]
    dot_general x48 -> x0, matrix products: 276 us -> none  [joined_rows(): jnp.dot(double_layer(piece, sources, moments), column_values, precision=l...]
    ppermute x100 -> x6, starting transfers between devices: 269 us -> 23.7 us  [shifted(): return lax.ppermute(x, axis, pairs)]
    ppermute x100 -> x6, waiting for transfers between devices: 146 us -> 10 us  [shifted(): return lax.ppermute(x, axis, pairs)]
    pallas_call x0 -> x8, Pallas kernels: none -> 108 us  [the longest x1 45 us: layer(): pl.pallas_call(layer_kernel, out_shape=shaped(1, 1536), in_specs=[SMEM] +...]
    another operation x3 -> x0, loops' own time: 97.1 us -> none  [the longest x1 94.8 us: local(): partial_sums = lax.map(joined_rows, row_starts).reshape(-1)]
    dynamic_slice x74 -> x3, local copies, waits for them, and re-layouts: 43.3 us -> 3.8 us  [the longest x1 2.28 us: local(): lax.dynamic_index_in_dim(grouped, row, 2, keepdims=False)]
    all_gather x3 -> x1, blocking collectives: 45.3 us -> 8.64 us  [local(): partials = lax.all_gather(partial, 'row', axis=0, tiled=True)]
  transfers between devices with their start and end apart: 103 -> 8, of which waited for: 50 -> 4; matrix products, arithmetic and copies ran while one was open for 2% -> 6% of each run, Pallas kernels for 0% -> 1%
where the time goes in v1:
time: 219 us; the launch traced here: 218 us
  Pallas kernels  108 us (49%)
  starting transfers between devices  41.9 us (19%)
  waiting for transfers between devices  26.3 us (12%)
  blocking collectives  22.6 us (10%)
  local copies, waits for them, and re-layouts  13.8 us (6%)
  other arithmetic  3.99 us (2%)
    pallas_call x1, Pallas kernels, layer(): pl.pallas_call(layer_kernel, out_shape=shaped(1, 1536), in_specs=[SMEM] +...  45 us
    pallas_call x1, Pallas kernels, second_solve(): pl.pallas_call(second_kernel, out_shape=shaped(CX, CY, CZ), in_specs=[SME...  32.3 us
    pallas_call x1, Pallas kernels, first_solve(): pl.pallas_call(first_kernel, out_shape=(shaped(CX, CY, CZ), shaped(4, 64,...  24.6 us
    ppermute x6, starting transfers between devices, shifted(): return lax.ppermute(x, axis, pairs)  23.7 us
    all_to_all x1, blocking collectives, local(): lax.all_to_all(reply, 'brick', split_axis=0, concat_axis=0, tiled=True)  13.9 us
    all_to_all x1, starting transfers between devices, local(): lax.all_to_all(message, ('row', 'brick'), split_axis=0, concat_axis=0, ti...  13.5 us
    ppermute x6, waiting for transfers between devices, shifted(): return lax.ppermute(x, axis, pairs)  10 us
    all_to_all x1, waiting for transfers between devices, local(): lax.all_to_all(message, ('row', 'brick'), split_axis=0, concat_axis=0, ti...  10 us
  transfers between devices with their start and end apart: 8, of which 4 were waited for; matrix products, arithmetic and copies ran while one was open for 6% of the time, Pallas kernels for 1%

profile of v1, /device:TPU:1, one launch (start us, length us, event | category | flops | bytes accessed | tf_op | source)
XLA Modules:
  0.0 217.9 jit_solution(7903270938970000872)
XLA Ops:
  0.6 1.1 copy-done.1
  1.8 0.3 own_source.1
  2.1 4.5 %collective-permute-start = (f32[10,40,256]{2,1,0:T(8,128)S(1)}, f32[10,40,256]{2,1,0:T(8,128)S(1)}, u32[]{:S(2)}, u32[]{:S(2)}) collective-permute-start(f32[10,40,256]{2,1,0:T(8,128)S(1)} %get-tuple-element.16.e_ref), channel_id=1, source_target_pairs={{0,4},{4,8},{8,12},{12,16},{16,20},{20,24},{24,28},{28,32},{32,36}... | collective-permute-start | bytes 1228808 | tf_op jit(solution)/shard_map/ppermute | solution.py:482
  6.6 1.3 collective-permute-start.1
  7.9 5.5 %collective-permute-start.2 = (f32[4,40,256]{2,1,0:T(8,128)S(1)}, f32[4,40,256]{2,1,0:T(8,128)S(1)}, u32[]{:S(2)}, u32[]{:S(2)}) collective-permute-start(f32[4,40,256]{2,1,0:T(8,128)S(1)} %get-tuple-element.17), channel_id=1, source_target_pairs={{0,8},{4,12},{8,16},{12,20},{16,24},{20,28},{24,32},{28,36},{32,40... | collective-permute-start | bytes 491528 | tf_op jit(solution)/shard_map/ppermute | solution.py:482
  13.4 1.3 collective-permute-start.3
  14.7 3.5 %collective-permute-done.2.l2_ref = f32[4,40,256]{2,1,0:T(8,128)S(1)} collective-permute-done((f32[4,40,256]{2,1,0:T(8,128)S(1)}, f32[4,40,256]{2,1,0:T(8,128)S(1)}, u32[]{:S(2)}, u32[]{:S(2)}) %collective-permute-start.2) | collective-permute-done | bytes 163872 | tf_op jit(solution)/shard_map/ppermute | solution.py:482
  18.3 6.5 %collective-permute-done.3.r2_ref = f32[4,40,256]{2,1,0:T(8,128)S(1)} collective-permute-done((f32[4,40,256]{2,1,0:T(8,128)S(1)}, f32[4,40,256]{2,1,0:T(8,128)S(1)}, u32[]{:S(2)}, u32[]{:S(2)}) %collective-permute-start.3) | collective-permute-done | bytes 163872 | tf_op jit(solution)/shard_map/ppermute | solution.py:482
  24.8 0.1 join_x.1
  24.9 9.2 %collective-permute-start.4 = (f32[30,16,256]{2,1,0:T(8,128)S(1)}, f32[30,16,256]{2,1,0:T(8,128)S(1)}, u32[]{:S(2)}, u32[]{:S(2)}) collective-permute-start(f32[30,16,256]{2,1,0:T(8,128)S(1)} %get-tuple-element.20), channel_id=1, source_target_pairs={{0,1},{1,2},{2,3},{4,5},{5,6},{6,7},{8,9},{9,10},{10,11},{12,13},{... | collective-permute-start | bytes 1474568 | tf_op jit(solution)/shard_map/ppermute | solution.py:482
  34.1 1.9 collective-permute-start.5
  36.1 3.7 %pad_maximum_fusion = f32[6,98304]{1,0:T(8,128)} fusion(f32[3,98304]{1,0:T(4,128)} %param.9, f32[3,98304]{1,0:T(4,128)S(1)} %copy-done.2), kind=kLoop, calls=%fused_computation | loop fusion | flops 589824 | bytes 4718592 | tf_op jit(solution)/shard_map/concatenate | solution.py:498
  40.0 0.8 dynamic_slice.12
  40.8 5.0 %reshape.26 = f32[6,64,4,384]{3,2,1,0:T(4,128)} reshape(f32[6,98304]{1,0:T(8,128)} %pad_maximum_fusion) | data formatting | bytes 4718592 | tf_op jit(solution)/shard_map/reshape | solution.py:498
  46.1 24.6 %first_solve.1 = (f32[8,32,256]{2,1,0:T(8,128)S(1)}, f32[4,64,36]{2,1,0:T(8,128)}) custom-call(s32[4]{0:T(128)S(1)} %pad_add_fusion.place_ref, f32[30,40,256]{2,1,0:T(8,128)S(1)} %get-tuple-element.19.sx_ref, f32[30,16,256]{2,1,0:T(8,128)S(1)} %collective-permute-done.4.below_ref, f32[30,16,256]{2,1,0:T(8,128)S(1)} %collective-permute-done.5.above_ref, ...), custom_call_target="tpu_custom_call" | custom-call | tf_op jit(solution)/shard_map/first_solve/pallas_call | solution.py:213
  70.6 13.5 %all-to-all-start = ((f32[256,1,36]{2,1,0:T(1,128)}), f32[256,1,36]{2,1,0:T(1,128)S(1)}, u32[]{:S(2)}, u32[]{:S(2)}) async-start(f32[256,1,36]{2,1,0:T(1,128)} %bitcast.9), calls=%async_computation | async-start | bytes 262144 | tf_op jit(solution)/shard_map/all_to_all | solution.py:511
  84.1 2.3 %constant_dynamic-slice_fusion = f32[6,64,1,384]{3,2,1,0:T(1,128)S(1)} fusion(f32[6,64,4,384]{3,2,1,0:T(4,128)} %reshape.26, s32[]{:T(128)S(6)} %select_n.22), kind=kLoop, calls=%fused_computation.15 | loop fusion | bytes 1179652 | tf_op jit(solution)/shard_map/jit(dynamic_index_in_dim)/dynamic_slice | solution.py:499
  86.5 0.4 copy.34
  86.8 10.0 %all-to-all-done = f32[256,1,36]{2,1,0:T(1,128)S(1)} async-done(((f32[256,1,36]{2,1,0:T(1,128)}), f32[256,1,36]{2,1,0:T(1,128)S(1)}, u32[]{:S(2)}, u32[]{:S(2)}) %all-to-all-start) | async-done | bytes 36896 | tf_op jit(solution)/shard_map/all_to_all | solution.py:511
  96.8 1.6 place_quarter.1
  98.5 0.7 copy.26
  99.2 4.6 %all-to-all-start.1 = ((f32[64,1,384]{2,1,0:T(1,128)}), f32[64,1,384]{2,1,0:T(1,128)S(1)}, u32[]{:S(2)}, u32[]{:S(2)}) async-start(f32[64,1,384]{2,1,0:T(1,128)} %copy.26), calls=%async_computation.1 | async-start | bytes 196608 | tf_op jit(solution)/shard_map/all_to_all | solution.py:513
  103.8 0.7 constant_dynamic-slice_fusion.1.target_ref
  104.6 2.7 %prepare.1 = (bf16[1536,48]{1,0:T(8,128)(2,1)S(1)}, bf16[48,24576]{1,0:T(8,128)(2,1)}, f32[8,24576]{1,0:T(8,128)S(1)}) custom-call(f32[3,1536]{1,0:T(4,128)S(1)} %constant_dynamic-slice_fusion.1.target_ref, f32[6,24576]{1,0:T(8,128)S(1)} %bitcast.40), custom_call_target="tpu_custom_call" | custom-call | tf_op jit(solution)/shard_map/prepare/pallas_call | solution.py:294
  107.3 6.3 %all-to-all-done.1 = f32[64,1,384]{2,1,0:T(1,128)S(1)} async-done(((f32[64,1,384]{2,1,0:T(1,128)}), f32[64,1,384]{2,1,0:T(1,128)S(1)}, u32[]{:S(2)}, u32[]{:S(2)}) %all-to-all-start.1) | async-done | bytes 98336 | tf_op jit(solution)/shard_map/all_to_all | solution.py:513
  113.6 1.7 copy-done
  115.2 45.0 %layer.1 = f32[1,1536]{1,0:T(1,128)S(1)} custom-call(s32[4]{0:T(128)S(1)} %pad_add_fusion.place_ref, bf16[1536,48]{1,0:T(8,128)(2,1)S(1)} %get-tuple-element.13.left_ref, bf16[48,24576]{1,0:T(8,128)(2,1)S(1)} %copy-done, f32[8,24576]{1,0:T(8,128)S(1)} %get-tuple-element.15.moment_ref, f32[64,384]{1,0:T(8,128)S(1)} %bitcast.47, ...), custom_call_target="tpu_custom_call" | custom-call | tf_op jit(solution)/shard_map/layer/pallas_call | solution.py:341
  160.2 8.6 %all-gather = f32[4,1,1536]{2,1,0:T(1,128)S(1)} all-gather(f32[1,1,1536]{2,1,0:T(1,128)S(1)} %bitcast.49), channel_id=1, replica_groups=mesh['brick'=64,'row'=4] {'row'}, dimensions={0}, use_global_device_ids=true | all-gather | bytes 30720 | tf_op jit(solution)/shard_map/all_gather | solution.py:515
  168.9 1.9 answer.1
  170.9 13.9 %all_to_all.33 = f32[64,1,384]{2,1,0:T(1,128)S(1)} all-to-all(f32[64,1,384]{2,1,0:T(1,128)S(1)} %copy.27), channel_id=1, replica_groups=mesh['brick'=64,'row'=4] {'brick'}, dimensions={0} | all-to-all | bytes 196608 | tf_op jit(solution)/shard_map/all_to_all | solution.py:517
  185.0 32.3 %second_solve.1 = f32[8,32,256]{2,1,0:T(8,128)} custom-call(s32[4]{0:T(128)S(1)} %pad_add_fusion.place_ref, f32[64,384]{1,0:T(8,128)S(1)} %bitcast.44, f32[8,32,256]{2,1,0:T(8,128)S(1)} %get-tuple-element.23.first_ref), custom_call_target="tpu_custom_call" | custom-call | tf_op jit(solution)/shard_map/second_solve/pallas_call | solution.py:468
  217.2 0.7 copy.28
  (31 shorter events, 0.8 us)
Async XLA Ops:
  0.6 1.1 copy-start.1
  1.8 34.3 %copy-start.2 = (f32[3,98304]{1,0:T(4,128)S(1)}, f32[3,98304]{1,0:T(4,128)}, u32[]{:S(2)}) copy-start(f32[3,98304]{1,0:T(4,128)} %param.8) | copy-start | bytes 3538948
  2.1 22.7 %collective-permute-start = (f32[10,40,256]{2,1,0:T(8,128)S(1)}, f32[10,40,256]{2,1,0:T(8,128)S(1)}, u32[]{:S(2)}, u32[]{:S(2)}) collective-permute-start(f32[10,40,256]{2,1,0:T(8,128)S(1)} %get-tuple-element.16.e_ref), channel_id=1, source_target_pairs={{0,4},{4,8},{8,12},{12,16},{16,20},{20,24},{24,28},{28,32},{32,36}... | collective-permute-start | bytes 1228808 | tf_op jit(solution)/shard_map/ppermute | solution.py:482
  6.6 18.1 %collective-permute-start.1 = (f32[10,40,256]{2,1,0:T(8,128)S(1)}, f32[10,40,256]{2,1,0:T(8,128)S(1)}, u32[]{:S(2)}, u32[]{:S(2)}) collective-permute-start(f32[10,40,256]{2,1,0:T(8,128)S(1)} %get-tuple-element.16.e_ref), channel_id=1, source_target_pairs={{4,0},{8,4},{12,8},{16,12},{20,16},{24,20},{28,24},{32,28},{36,32}... | collective-permute-start | bytes 1228808 | tf_op jit(solution)/shard_map/ppermute | solution.py:482
  7.9 10.3 %collective-permute-start.2 = (f32[4,40,256]{2,1,0:T(8,128)S(1)}, f32[4,40,256]{2,1,0:T(8,128)S(1)}, u32[]{:S(2)}, u32[]{:S(2)}) collective-permute-start(f32[4,40,256]{2,1,0:T(8,128)S(1)} %get-tuple-element.17), channel_id=1, source_target_pairs={{0,8},{4,12},{8,16},{12,20},{16,24},{20,28},{24,32},{28,36},{32,40... | collective-permute-start | bytes 491528 | tf_op jit(solution)/shard_map/ppermute | solution.py:482
  13.4 11.3 %collective-permute-start.3 = (f32[4,40,256]{2,1,0:T(8,128)S(1)}, f32[4,40,256]{2,1,0:T(8,128)S(1)}, u32[]{:S(2)}, u32[]{:S(2)}) collective-permute-start(f32[4,40,256]{2,1,0:T(8,128)S(1)} %get-tuple-element.18), channel_id=1, source_target_pairs={{8,0},{12,4},{16,8},{20,12},{24,16},{28,20},{32,24},{36,28},{40,32... | collective-permute-start | bytes 491528 | tf_op jit(solution)/shard_map/ppermute | solution.py:482
  24.9 21.1 %collective-permute-start.4 = (f32[30,16,256]{2,1,0:T(8,128)S(1)}, f32[30,16,256]{2,1,0:T(8,128)S(1)}, u32[]{:S(2)}, u32[]{:S(2)}) collective-permute-start(f32[30,16,256]{2,1,0:T(8,128)S(1)} %get-tuple-element.20), channel_id=1, source_target_pairs={{0,1},{1,2},{2,3},{4,5},{5,6},{6,7},{8,9},{9,10},{10,11},{12,13},{... | collective-permute-start | bytes 1474568 | tf_op jit(solution)/shard_map/ppermute | solution.py:482
  34.1 5.6 %copy-start.3 = (s32[1,1,64,12]{2,1,3,0:T(1,128)S(1)}, s32[1,1,64,12]{2,1,3,0:T(1,128)}, u32[]{:S(2)}) copy-start(s32[1,1,64,12]{2,1,3,0:T(1,128)} %param.11) | copy-start | bytes 9220
  34.1 5.7 %copy-start.4 = (s32[1,1,64,12]{2,1,3,0:T(1,128)S(1)}, s32[1,1,64,12]{2,1,3,0:T(1,128)}, u32[]{:S(2)}) copy-start(s32[1,1,64,12]{2,1,3,0:T(1,128)} %param.12) | copy-start | bytes 9220
  34.1 11.9 %collective-permute-start.5 = (f32[30,16,256]{2,1,0:T(8,128)S(1)}, f32[30,16,256]{2,1,0:T(8,128)S(1)}, u32[]{:S(2)}, u32[]{:S(2)}) collective-permute-start(f32[30,16,256]{2,1,0:T(8,128)S(1)} %get-tuple-element.21), channel_id=1, source_target_pairs={{1,0},{2,1},{3,2},{5,4},{6,5},{7,6},{9,8},{10,9},{11,10},{13,12},{... | collective-permute-start | bytes 1474568 | tf_op jit(solution)/shard_map/ppermute | solution.py:482
  40.8 5.1 %copy-start.5 = (s32[1,1,64]{2,1,0:T(1,128)S(1)}, s32[1,1,64]{2,1,0:T(1,128)}, u32[]{:S(2)}) copy-start(s32[1,1,64]{2,1,0:T(1,128)} %param.13) | copy-start | bytes 772
  70.6 26.2 %all-to-all-start = ((f32[256,1,36]{2,1,0:T(1,128)}), f32[256,1,36]{2,1,0:T(1,128)S(1)}, u32[]{:S(2)}, u32[]{:S(2)}) async-start(f32[256,1,36]{2,1,0:T(1,128)} %bitcast.9), calls=%async_computation | async-start | bytes 262144 | tf_op jit(solution)/shard_map/all_to_all | solution.py:511
  99.2 14.4 %all-to-all-start.1 = ((f32[64,1,384]{2,1,0:T(1,128)}), f32[64,1,384]{2,1,0:T(1,128)S(1)}, u32[]{:S(2)}, u32[]{:S(2)}) async-start(f32[64,1,384]{2,1,0:T(1,128)} %copy.26), calls=%async_computation.1 | async-start | bytes 196608 | tf_op jit(solution)/shard_map/all_to_all | solution.py:513
  113.6 1.7 copy-start

commit v2 on v1

--- a/solution.py
+++ b/solution.py
@@ -22,6 +22,7 @@
 XS = CX + 22
 XD = CX + 24
 HALF = 128
+RIM = CY + 2
 PARAMS = pltpu.CompilerParams(vmem_limit_bytes=50 * 1024 * 1024)
 DEAD_SLOT = 4096
 TINY = 1e-30
@@ -71,7 +72,7 @@
     return dn, up
 
 
-def source_kernel(m_ref, e_ref, low_ref, high_ref, pad):
+def source_kernel(m_ref, e_ref, flat_ref, low_ref, high_ref, pad):
     pad[...] = jnp.zeros_like(pad)
     for x in range(CX):
         pad[0, x + 1, 12:44, :] = m_ref[0, x]
@@ -89,41 +90,68 @@
             total = total + jnp.concatenate([up[0] - dn[0], up[1] - dn[1]], axis=1)
         total = -0.5 * total
         e_ref[i] = total
+        rim = e_ref[i, 3:37, :]
+        flat_ref[i * RIM : (i + 1) * RIM, :] = rim
         if i < 4:
-            low_ref[i] = total
-        if i >= CX - 2:
-            high_ref[i - (CX - 2)] = total
+            low_ref[i * RIM : (i + 1) * RIM, :] = rim
+        j = i - (CX - 2)
+        if j >= 0:
+            high_ref[j * RIM : (j + 1) * RIM, :] = rim
 
 
 def own_source(magnet):
     return pl.pallas_call(
         source_kernel,
-        out_shape=(shaped(10, 40, CZ), shaped(4, 40, CZ), shaped(4, 40, CZ)),
+        out_shape=(
+            shaped(10, 40, CZ),
+            shaped(10 * RIM, CZ),
+            shaped(4 * RIM, CZ),
+            shaped(4 * RIM, CZ),
+        ),
         in_specs=[VMEM],
-        out_specs=(VMEM, VMEM, VMEM),
+        out_specs=(VMEM,) * 4,
         scratch_shapes=[pltpu.VMEM((3, CX + 2, 56, CZ), F32)],
         compiler_params=PARAMS,
         name="own_source",
     )(magnet)
 
 
+def beside(plane, before, own):
+    return max(before - plane, plane - (before + own - 1), 0)
+
+
+def y_rows():
+    counts = [CX + 4 - beside(plane, 11, CX) for plane in range(XS)]
+    begins = [sum(counts[:plane]) for plane in range(XS)]
+    return counts, begins, -(-sum(counts) // 8) * 8
+
+
+Y_COUNTS, Y_BEGINS, Y_TOTAL = y_rows()
+
+
 def join_kernel(e_ref, l1_ref, r1_ref, l2_ref, r2_ref, sx_ref, upper_ref, lower_ref):
-    parts = ((e_ref, 10, 10), (l1_ref, 2, 10), (r1_ref, 18, 10), (l2_ref, 0, 4), (r2_ref, 26, 4))
+    parts = ((l1_ref, 2, 10), (r1_ref, 18, 10), (l2_ref, 0, 4), (r2_ref, 26, 4))
+    upper_ref[Y_TOTAL - 8 :, :] = jnp.zeros((8, CZ), F32)
+    lower_ref[Y_TOTAL - 8 :, :] = jnp.zeros((8, CZ), F32)
     for plane in range(XS):
-        total = None
+        own = 10 <= plane < 20
+        sx_ref[plane] = e_ref[plane - 10] if own else jnp.zeros((40, CZ), F32)
+        total = sx_ref[plane, 3:37, :] if own else None
         for ref, begin, count in parts:
             if begin <= plane < begin + count:
-                term = ref[plane - begin]
+                at = (plane - begin) * RIM
+                term = ref[at : at + RIM, :]
                 total = term if total is None else total + term
-        sx_ref[plane] = total
-        upper_ref[plane] = total[24:40]
-        lower_ref[plane] = total[0:16]
+        sx_ref[plane, 3:37, :] = total
+        rows, at = Y_COUNTS[plane], Y_BEGINS[plane]
+        upper_ref[at : at + rows, :] = sx_ref[plane, 37 - rows : 37, :]
+        lower_ref[at : at + rows, :] = sx_ref[plane, 3 : 3 + rows, :]
 
 
 def join_x(own, l1, r1, l2, r2):
     return pl.pallas_call(
         join_kernel,
-        out_shape=(shaped(XS, 40, CZ), shaped(XS, 16, CZ), shaped(XS, 16, CZ)),
+        out_shape=(shaped(XS, 40, CZ), shaped(Y_TOTAL, CZ), shaped(Y_TOTAL, CZ)),
         in_specs=[VMEM] * 5,
         out_specs=(VMEM,) * 3,
         compiler_params=PARAMS,
@@ -131,15 +159,20 @@
     )(own, l1, r1, l2, r2)
 
 
-def neighbours(src, x):
-    c = src[x]
-    around_x = src[x - 1] + src[x + 1]
+def plane_rows(reach):
+    return (0, YE) if reach > 3 else (8, YE - 8)
+
+
+def neighbours(src, x, rows):
+    begin, end = rows
+    c = src[x, begin:end, :]
+    around_x = src[x - 1, begin:end, :] + src[x + 1, begin:end, :]
     halves = (c[:, :HALF], c[:, HALF:])
     dn, up = z_pair(*halves)
     out = []
     for h in range(2):
         v = halves[h]
-        around_y = pltpu.roll(v, 1, 0) + pltpu.roll(v, YE - 1, 0)
+        around_y = pltpu.roll(v, 1, 0) + pltpu.roll(v, end - begin - 1, 0)
         around = around_x[:, h * HALF : (h + 1) * HALF] + around_y + (dn[h] + up[h])
         out.append((v, around))
     return out
@@ -155,33 +188,30 @@
         at = brick * CX + x - 11
         return jnp.where((at >= 0) & (at < cells_x), scale, 0.0).astype(F32)
 
-    def gather_plane(x, carry):
-        t = sx_ref[x]
-        lo = below_ref[x]
-        hi = above_ref[x]
-        full = jnp.concatenate(
-            [lo[0:8], t[0:8] + lo[8:16], t[8:32], t[32:40] + hi[0:8], hi[8:16]], axis=0
-        )
-        s[x] = full
+    edge = jnp.zeros((8, CZ), F32)
+    for x in range(XS):
+        s[x, 0:8, :] = edge
+        s[x, 48:56, :] = edge
+        s[x, 8:48, :] = sx_ref[x]
+        rows, at = Y_COUNTS[x], Y_BEGINS[x]
+        s[x, 13 - rows : 13, :] += below_ref[at : at + rows, :]
+        s[x, 43 : 43 + rows, :] += above_ref[at : at + rows, :]
         coef = in_y * x_scale(x, WEIGHTS[0] / 6.0)
+        full = s[x]
         buf[0, x, :, :HALF] = coef * full[:, :HALF]
         buf[0, x, :, HALF:] = coef * full[:, HALF:]
-        return carry
-
-    lax.fori_loop(0, XS, gather_plane, 0)
     for k in range(1, SWEEPS):
         weight = WEIGHTS[k]
         src, dst = buf.at[(k - 1) % 2], buf.at[k % 2]
 
-        def plane(x, carry, src=src, dst=dst, weight=weight):
-            coef = in_y * x_scale(x, weight / 6.0)
-            source = s[x]
-            for h, (v, around) in enumerate(neighbours(src, x)):
+        for x in range(k, XS - k):
+            rows = plane_rows(SWEEPS - 1 - k - beside(x, 11, CX))
+            begin, end = rows
+            coef = in_y[begin:end] * x_scale(x, weight / 6.0)
+            source = s[x, begin:end, :]
+            for h, (v, around) in enumerate(neighbours(src, x, rows)):
                 lanes = slice(h * HALF, (h + 1) * HALF)
-                dst[x, :, lanes] = (1.0 - weight) * v + coef * (source[:, lanes] + around)
-            return carry
-
-        lax.fori_loop(k, XS - k, plane, 0)
+                dst[x, begin:end, lanes] = (1.0 - weight) * v + coef * (source[:, lanes] + around)
     last = (SWEEPS - 1) % 2
     for x in range(CX):
         field_ref[x] = buf[last, x + 11, YO : YO + CY, :]
@@ -246,6 +276,8 @@
 
 
 SRC = 24576
+BLOCK = 1536
+QUARTER = 384
 CHUNK = 768
 TILE = 128
 
@@ -259,14 +291,15 @@
 LEFT = (0, 0, 0, 1, 1, 2)
 
 
-def prepare_kernel(target_ref, source_ref, left_ref, right_ref, moment_ref):
-    sub = lax.broadcasted_iota(jnp.int32, (8, CHUNK), 0)
-
-    def sources(c, carry):
-        at = pl.multiple_of(c * CHUNK, CHUNK)
-        v = source_ref[:, pl.ds(at, CHUNK)]
-        pos = v[0:3] - 4.0
-        mom = v[3:6]
+def prepare_kernel(place_ref, position_ref, moment_ref, left_ref, right_ref, face_ref):
+    brick, row = place_ref[0], place_ref[1]
+    sub = lax.broadcasted_iota(jnp.int32, (8, QUARTER), 0)
+
+    def sources(b, carry):
+        node = pl.multiple_of(b * BLOCK + row * QUARTER, HALF)
+        at = pl.multiple_of(b * QUARTER, HALF)
+        pos = position_ref[:, pl.ds(node, QUARTER)] - 4.0
+        mom = moment_ref[:, pl.ds(node, QUARTER)]
         norm = jnp.sum(pos * pos, axis=0, keepdims=True)
         across = jnp.sum(pos * mom, axis=0, keepdims=True)
         dist = jnp.where(sub == 3, 1.0, jnp.where(sub == 4, norm, 0.0))
@@ -274,14 +307,15 @@
         for i in range(3):
             dist = jnp.where(sub == i, -2.0 * pos[i : i + 1], dist)
             face = jnp.where(sub == i, mom[i : i + 1], face)
-        right_ref[:, pl.ds(at, CHUNK)] = stack_six(dist, RIGHT).astype(BF16)
-        moment_ref[:, pl.ds(at, CHUNK)] = face
+        right_ref[:, pl.ds(at, QUARTER)] = stack_six(dist, RIGHT).astype(BF16)
+        face_ref[:, pl.ds(at, QUARTER)] = face
         return carry
 
-    lax.fori_loop(0, SRC // CHUNK, sources, 0)
+    lax.fori_loop(0, SRC // QUARTER, sources, 0, unroll=2)
     sub = lax.broadcasted_iota(jnp.int32, (8, TILE), 0)
-    for t in range(1536 // TILE):
-        pos = target_ref[0:3, t * TILE : (t + 1) * TILE] - 4.0
+    for t in range(BLOCK // TILE):
+        node = pl.multiple_of(brick * BLOCK + t * TILE, HALF)
+        pos = position_ref[:, pl.ds(node, TILE)] - 4.0
         norm = jnp.sum(pos * pos, axis=0, keepdims=True) + SOFTENING
         feat = jnp.where(sub == 3, norm, jnp.where(sub == 4, 1.0, 0.0))
         for i in range(3):
@@ -290,15 +324,15 @@
         left_ref[t * TILE : (t + 1) * TILE, :] = rows.T[:, :48].astype(BF16)
 
 
-def prepare(targets, sources):
+def prepare(place, position, moment):
     return pl.pallas_call(
         prepare_kernel,
-        out_shape=(shaped(1536, 48, dtype=BF16), shaped(48, SRC, dtype=BF16), shaped(8, SRC)),
-        in_specs=[VMEM, VMEM],
+        out_shape=(shaped(BLOCK, 48, dtype=BF16), shaped(48, SRC, dtype=BF16), shaped(8, SRC)),
+        in_specs=[SMEM, VMEM, VMEM],
         out_specs=(VMEM, VMEM, VMEM),
         compiler_params=PARAMS,
         name="prepare",
-    )(targets, sources)
+    )(place, position, moment)
 
 
 def layer_kernel(place_ref, left_ref, right_ref, moment_ref, trace_ref, fraction_ref, out_ref, acc):
@@ -452,14 +486,13 @@
         weight = WEIGHTS[k - 1]
         src, dst = buf.at[(k - 1) % 2], buf.at[k % 2]
 
-        def plane(x, carry, src=src, dst=dst, weight=weight):
-            free = mask[x]
-            for h, (v, around) in enumerate(neighbours(src, x)):
+        for x in range(k, XD - k):
+            rows = plane_rows(SWEEPS - k - beside(x, YO, CX))
+            begin, end = rows
+            free = mask[x, begin:end, :]
+            for h, (v, around) in enumerate(neighbours(src, x, rows)):
                 lanes = slice(h * HALF, (h + 1) * HALF)
-                dst[x, :, lanes] = v + free[:, lanes] * ((weight / 6.0) * around - weight * v)
-            return carry
-
-        lax.fori_loop(k, XD - k, plane, 0)
+                dst[x, begin:end, lanes] = v + free[:, lanes] * ((weight / 6.0) * around - weight * v)
     for x in range(CX):
         out_ref[x] = first_ref[x] + buf[SWEEPS % 2, x + YO, YO : YO + CY, :]
 
@@ -495,14 +528,11 @@
     cell_f = jnp.where(live, cell, -1).astype(F32)
     base = jnp.concatenate([slot_f, zeros, cell_f], axis=1)
     cells = cell.T.reshape(2, 6, bricks).transpose(1, 0, 2).reshape(6, 2 * bricks)
-    grouped = jnp.concatenate([node_position, node_moment], axis=0).reshape(6, bricks, rows, 384)
-    sources = lax.dynamic_index_in_dim(grouped, row, 2, keepdims=False).reshape(6, bricks * 384)
-    targets = lax.dynamic_slice_in_dim(node_position, brick * 1536, 1536, 1)
     fraction = lax.dynamic_slice_in_dim(solid_fraction, brick * 1536 + row * 384, 384, 0)[None]
-    left, right, moment = prepare(targets, sources)
-
-    own, low, high = own_source(magnet)
-    l1, r1 = shifted(own, "brick", 1), shifted(own, "brick", -1)
+    left, right, moment = prepare(place, node_position, node_moment)
+
+    own, flat, low, high = own_source(magnet)
+    l1, r1 = shifted(flat, "brick", 1), shifted(flat, "brick", -1)
     l2, r2 = shifted(high, "brick", 2), shifted(low, "brick", -2)
     sx, upper, lower = join_x(own, l1, r1, l2, r2)
     below, above = shifted(upper, "row", 1), shifted(lower, "row", -1)

time: 219 us -> 179 us (0.82)
  Pallas kernels: 108 us -> 74.3 us
  blocking collectives: 22.6 us -> 48.9 us
  starting transfers between devices: 41.9 us -> 25.9 us
  waiting for transfers between devices: 26.3 us -> 19.8 us
  local copies, waits for them, and re-layouts: 13.8 us -> 8.4 us
  other arithmetic: 3.99 us -> 0.31 us
    all_to_all x0 -> x1, blocking collectives: none -> 25.5 us  [local(): lax.all_to_all(message, ('row', 'brick'), split_axis=0, concat_axis=0, ti...]
    pallas_call x1, Pallas kernels: 32.3 us -> 13 us  [second_solve(): pl.pallas_call(second_kernel, out_shape=shaped(CX, CY, CZ), in_specs=[SME...]
    pallas_call x1, Pallas kernels: 24.6 us -> 7.29 us  [first_solve(): pl.pallas_call(first_kernel, out_shape=(shaped(CX, CY, CZ), shaped(4, 64,...]
    all_to_all x1 -> x0, starting transfers between devices: 13.5 us -> none  [local(): lax.all_to_all(message, ('row', 'brick'), split_axis=0, concat_axis=0, ti...]
    all_to_all x1 -> x0, waiting for transfers between devices: 10 us -> none  [local(): lax.all_to_all(message, ('row', 'brick'), split_axis=0, concat_axis=0, ti...]
    ppermute x6, waiting for transfers between devices: 10 us -> 15.2 us  [shifted(): return lax.ppermute(x, axis, pairs)]
    reshape x1 -> x0, local copies, waits for them, and re-layouts: 4.97 us -> none  [local(): jnp.concatenate([node_position, node_moment], axis=0)]
    concatenate x1 -> x0, other arithmetic: 3.67 us -> none  [local(): jnp.concatenate([node_position, node_moment], axis=0)]
  transfers between devices with their start and end apart: 8 -> 7, of which waited for: 4 -> 5; matrix products, arithmetic and copies ran while one was open for 6% -> 1% of each run, Pallas kernels for 1% -> 2%
where the time goes in v2:
time: 179 us; the launch traced here: 178 us
  Pallas kernels  74.3 us (42%)
  blocking collectives  48.9 us (27%)
  starting transfers between devices  25.9 us (14%)
  waiting for transfers between devices  19.8 us (11%)
  local copies, waits for them, and re-layouts  8.4 us (5%)
    pallas_call x1, Pallas kernels, layer(): pl.pallas_call(layer_kernel, out_shape=shaped(1, 1536), in_specs=[SMEM] +...  45 us
    all_to_all x1, blocking collectives, local(): lax.all_to_all(message, ('row', 'brick'), split_axis=0, concat_axis=0, ti...  25.5 us
    ppermute x6, starting transfers between devices, shifted(): return lax.ppermute(x, axis, pairs)  21.1 us
    ppermute x6, waiting for transfers between devices, shifted(): return lax.ppermute(x, axis, pairs)  15.2 us
    all_to_all x1, blocking collectives, local(): lax.all_to_all(reply, 'brick', split_axis=0, concat_axis=0, tiled=True)  14.9 us
    pallas_call x1, Pallas kernels, second_solve(): pl.pallas_call(second_kernel, out_shape=shaped(CX, CY, CZ), in_specs=[SME...  13 us
    all_gather x1, blocking collectives, local(): partials = lax.all_gather(partial, 'row', axis=0, tiled=True)  8.46 us
    pallas_call x1, Pallas kernels, first_solve(): pl.pallas_call(first_kernel, out_shape=(shaped(CX, CY, CZ), shaped(4, 64,...  7.29 us
  transfers between devices with their start and end apart: 7, of which 5 were waited for; matrix products, arithmetic and copies ran while one was open for 1% of the time, Pallas kernels for 2%

profile of v2, /device:TPU:1, one launch (start us, length us, event | category | flops | bytes accessed | tf_op | source)
XLA Modules:
  0.0 178.4 jit_solution(15303929367595878295)
XLA Ops:
  0.6 1.1 copy-done.2
  1.8 0.3 own_source.1
  2.1 1.3 collective-permute-start.1
  3.4 5.0 %collective-permute-start = (f32[340,256]{1,0:T(8,128)S(1)}, f32[340,256]{1,0:T(8,128)S(1)}, u32[]{:S(2)}, u32[]{:S(2)}) collective-permute-start(f32[340,256]{1,0:T(8,128)S(1)} %get-tuple-element.18), channel_id=1, source_target_pairs={{0,4},{4,8},{8,12},{12,16},{16,20},{20,24},{24,28},{28,32},{32,36}... | collective-permute-start | bytes 1044488 | tf_op jit(solution)/shard_map/ppermute | solution.py:515
  8.4 4.9 %collective-permute-start.2 = (f32[136,256]{1,0:T(8,128)S(1)}, f32[136,256]{1,0:T(8,128)S(1)}, u32[]{:S(2)}, u32[]{:S(2)}) collective-permute-start(f32[136,256]{1,0:T(8,128)S(1)} %get-tuple-element.19), channel_id=1, source_target_pairs={{0,8},{4,12},{8,16},{12,20},{16,24},{20,28},{24,32},{28,36},{32,40... | collective-permute-start | bytes 417800 | tf_op jit(solution)/shard_map/ppermute | solution.py:515
  13.3 1.3 collective-permute-start.3
  14.6 0.8 copy.21
  15.4 0.8 copy.18
  16.2 0.7 collective-permute-done.2.l2_ref
  16.9 7.7 %collective-permute-done.3.r2_ref = f32[136,256]{1,0:T(8,128)S(1)} collective-permute-done((f32[136,256]{1,0:T(8,128)S(1)}, f32[136,256]{1,0:T(8,128)S(1)}, u32[]{:S(2)}, u32[]{:S(2)}) %collective-permute-start.3) | collective-permute-done | bytes 139296 | tf_op jit(solution)/shard_map/ppermute | solution.py:515
  24.6 1.0 join_x.1
  25.6 6.7 %collective-permute-start.4 = (f32[232,256]{1,0:T(8,128)}, f32[232,256]{1,0:T(8,128)S(1)}, u32[]{:S(2)}, u32[]{:S(2)}) collective-permute-start(f32[232,256]{1,0:T(8,128)} %get-tuple-element.22), channel_id=1, source_target_pairs={{0,1},{1,2},{2,3},{4,5},{5,6},{6,7},{8,9},{9,10},{10,11},{12,13},{... | collective-permute-start | bytes 712712 | tf_op jit(solution)/shard_map/ppermute | solution.py:515
  32.3 1.9 %collective-permute-start.5 = (f32[232,256]{1,0:T(8,128)}, f32[232,256]{1,0:T(8,128)S(1)}, u32[]{:S(2)}, u32[]{:S(2)}) collective-permute-start(f32[232,256]{1,0:T(8,128)} %get-tuple-element.23), channel_id=1, source_target_pairs={{1,0},{2,1},{3,2},{5,4},{6,5},{7,6},{9,8},{10,9},{11,10},{13,12},{... | collective-permute-start | bytes 712712 | tf_op jit(solution)/shard_map/ppermute | solution.py:515
  34.6 1.0 collective-permute-done.4.below_ref
  35.7 5.8 %collective-permute-done.5.above_ref = f32[232,256]{1,0:T(8,128)S(1)} collective-permute-done((f32[232,256]{1,0:T(8,128)}, f32[232,256]{1,0:T(8,128)S(1)}, u32[]{:S(2)}, u32[]{:S(2)}) %collective-permute-start.5) | collective-permute-done | bytes 237600 | tf_op jit(solution)/shard_map/ppermute | solution.py:515
  41.5 0.7 copy-done.3
  42.1 0.9 copy-done.4
  43.1 7.3 %first_solve.1 = (f32[8,32,256]{2,1,0:T(8,128)S(1)}, f32[4,64,36]{2,1,0:T(8,128)S(1)}) custom-call(s32[4]{0:T(128)S(1)} %pad_add_fusion.place_ref, f32[30,40,256]{2,1,0:T(8,128)S(1)} %get-tuple-element.21.sx_ref, f32[232,256]{1,0:T(8,128)S(1)} %collective-permute-done.4.below_ref, f32[232,256]{1,0:T(8,128)S(1)} %copy-done.4, s32[6,128]{1,0:T(8,128)S(1)} %reshape.20.cell_ref, ...), custom_call_target="tpu_custom_call" | custom-call | tf_op jit(solution)/shard_map/first_solve/pallas_call | solution.py:243
  50.4 25.5 %all_to_all.33 = f32[256,1,36]{2,1,0:T(1,128)S(1)} all-to-all(f32[256,1,36]{2,1,0:T(1,128)S(1)} %bitcast.41), channel_id=1, replica_groups=mesh['brick'=64,'row'=4] {'row','brick'}, dimensions={0} | all-to-all | bytes 73728 | tf_op jit(solution)/shard_map/all_to_all | solution.py:541
  75.9 1.6 place_quarter.1
  77.5 0.7 copy.23
  78.3 4.8 %all-to-all-start.1 = ((f32[64,1,384]{2,1,0:T(1,128)}), f32[64,1,384]{2,1,0:T(1,128)S(1)}, u32[]{:S(2)}, u32[]{:S(2)}) async-start(f32[64,1,384]{2,1,0:T(1,128)} %copy.23), calls=%async_computation.1 | async-start | bytes 196608 | tf_op jit(solution)/shard_map/all_to_all | solution.py:543
  83.1 0.8 dynamic_slice.3
  83.9 4.2 %prepare.1 = (bf16[1536,48]{1,0:T(8,128)(2,1)S(1)}, bf16[48,24576]{1,0:T(8,128)(2,1)}, f32[8,24576]{1,0:T(8,128)S(1)}) custom-call(s32[4]{0:T(128)S(1)} %pad_add_fusion.place_ref, f32[3,98304]{1,0:T(4,128)S(1)} %copy-done.1, f32[3,98304]{1,0:T(4,128)} %moment_ref.1), custom_call_target="tpu_custom_call" | custom-call | tf_op jit(solution)/shard_map/prepare/pallas_call | solution.py:328
  88.1 4.5 %all-to-all-done.1 = f32[64,1,384]{2,1,0:T(1,128)S(1)} async-done(((f32[64,1,384]{2,1,0:T(1,128)}), f32[64,1,384]{2,1,0:T(1,128)S(1)}, u32[]{:S(2)}, u32[]{:S(2)}) %all-to-all-start.1) | async-done | bytes 98336 | tf_op jit(solution)/shard_map/all_to_all | solution.py:543
  92.6 1.7 copy-done
  94.3 45.0 %layer.1 = f32[1,1536]{1,0:T(1,128)S(1)} custom-call(s32[4]{0:T(128)S(1)} %pad_add_fusion.place_ref, bf16[1536,48]{1,0:T(8,128)(2,1)S(1)} %get-tuple-element.14.left_ref, bf16[48,24576]{1,0:T(8,128)(2,1)S(1)} %copy-done, f32[8,24576]{1,0:T(8,128)S(1)} %get-tuple-element.16.moment_ref, f32[64,384]{1,0:T(8,128)S(1)} %bitcast.40, ...), custom_call_target="tpu_custom_call" | custom-call | tf_op jit(solution)/shard_map/layer/pallas_call | solution.py:375
  139.3 8.5 %all-gather = f32[4,1,1536]{2,1,0:T(1,128)S(1)} all-gather(f32[1,1,1536]{2,1,0:T(1,128)S(1)} %bitcast.43), channel_id=1, replica_groups=mesh['brick'=64,'row'=4] {'row'}, dimensions={0}, use_global_device_ids=true | all-gather | bytes 30720 | tf_op jit(solution)/shard_map/all_gather | solution.py:545
  147.7 1.9 %answer.1 = f32[64,384]{1,0:T(8,128)S(1)} custom-call(s32[4]{0:T(128)S(1)} %pad_add_fusion.place_ref, f32[4,1536]{1,0:T(4,128)S(1)} %bitcast.42, f32[256,36]{1,0:T(8,128)S(1)} %bitcast.35), custom_call_target="tpu_custom_call" | custom-call | tf_op jit(solution)/shard_map/answer/pallas_call | solution.py:419
  149.8 14.9 %all_to_all.34 = f32[64,1,384]{2,1,0:T(1,128)S(1)} all-to-all(f32[64,1,384]{2,1,0:T(1,128)S(1)} %copy.24), channel_id=1, replica_groups=mesh['brick'=64,'row'=4] {'brick'}, dimensions={0} | all-to-all | bytes 196608 | tf_op jit(solution)/shard_map/all_to_all | solution.py:547
  164.8 13.0 %second_solve.1 = f32[8,32,256]{2,1,0:T(8,128)} custom-call(s32[4]{0:T(128)S(1)} %pad_add_fusion.place_ref, f32[64,384]{1,0:T(8,128)S(1)} %bitcast.37, f32[8,32,256]{2,1,0:T(8,128)S(1)} %get-tuple-element.25.first_ref), custom_call_target="tpu_custom_call" | custom-call | tf_op jit(solution)/shard_map/second_solve/pallas_call | solution.py:501
  177.7 0.7 copy.25
  (26 shorter events, 0.6 us)
Async XLA Ops:
  0.6 1.1 copy-start.2
  1.8 32.5 %copy-start.6 = (s32[1,1,64]{2,1,0:T(1,128)S(1)}, s32[1,1,64]{2,1,0:T(1,128)}, u32[]{:S(2)}) copy-start(s32[1,1,64]{2,1,0:T(1,128)} %param.13) | copy-start | bytes 772
  1.8 32.6 %copy-start.5 = (s32[1,1,64,12]{2,1,3,0:T(1,128)S(1)}, s32[1,1,64,12]{2,1,3,0:T(1,128)}, u32[]{:S(2)}) copy-start(s32[1,1,64,12]{2,1,3,0:T(1,128)} %param.11) | copy-start | bytes 9220
  2.1 22.5 %collective-permute-start.1 = (f32[340,256]{1,0:T(8,128)S(1)}, f32[340,256]{1,0:T(8,128)S(1)}, u32[]{:S(2)}, u32[]{:S(2)}) collective-permute-start(f32[340,256]{1,0:T(8,128)S(1)} %get-tuple-element.18), channel_id=1, source_target_pairs={{4,0},{8,4},{12,8},{16,12},{20,16},{24,20},{28,24},{32,28},{36,32}... | collective-permute-start | bytes 1044488 | tf_op jit(solution)/shard_map/ppermute | solution.py:515
  3.4 21.2 %collective-permute-start = (f32[340,256]{1,0:T(8,128)S(1)}, f32[340,256]{1,0:T(8,128)S(1)}, u32[]{:S(2)}, u32[]{:S(2)}) collective-permute-start(f32[340,256]{1,0:T(8,128)S(1)} %get-tuple-element.18), channel_id=1, source_target_pairs={{0,4},{4,8},{8,12},{12,16},{16,20},{20,24},{24,28},{28,32},{32,36}... | collective-permute-start | bytes 1044488 | tf_op jit(solution)/shard_map/ppermute | solution.py:515
  8.4 8.4 %collective-permute-start.2 = (f32[136,256]{1,0:T(8,128)S(1)}, f32[136,256]{1,0:T(8,128)S(1)}, u32[]{:S(2)}, u32[]{:S(2)}) collective-permute-start(f32[136,256]{1,0:T(8,128)S(1)} %get-tuple-element.19), channel_id=1, source_target_pairs={{0,8},{4,12},{8,16},{12,20},{16,24},{20,28},{24,32},{28,36},{32,40... | collective-permute-start | bytes 417800 | tf_op jit(solution)/shard_map/ppermute | solution.py:515
  13.3 11.3 %collective-permute-start.3 = (f32[136,256]{1,0:T(8,128)S(1)}, f32[136,256]{1,0:T(8,128)S(1)}, u32[]{:S(2)}, u32[]{:S(2)}) collective-permute-start(f32[136,256]{1,0:T(8,128)S(1)} %get-tuple-element.20), channel_id=1, source_target_pairs={{8,0},{12,4},{16,8},{20,12},{24,16},{28,20},{32,24},{36,28},{40,32... | collective-permute-start | bytes 417800 | tf_op jit(solution)/shard_map/ppermute | solution.py:515
  25.6 58.2 %copy-start.1 = (f32[3,98304]{1,0:T(4,128)S(1)}, f32[3,98304]{1,0:T(4,128)}, u32[]{:S(2)}) copy-start(f32[3,98304]{1,0:T(4,128)} %position_ref.1) | copy-start | bytes 3538948
  25.6 10.0 %collective-permute-start.4 = (f32[232,256]{1,0:T(8,128)}, f32[232,256]{1,0:T(8,128)S(1)}, u32[]{:S(2)}, u32[]{:S(2)}) collective-permute-start(f32[232,256]{1,0:T(8,128)} %get-tuple-element.22), channel_id=1, source_target_pairs={{0,1},{1,2},{2,3},{4,5},{5,6},{6,7},{8,9},{9,10},{10,11},{12,13},{... | collective-permute-start | bytes 712712 | tf_op jit(solution)/shard_map/ppermute | solution.py:515
  32.3 9.1 %collective-permute-start.5 = (f32[232,256]{1,0:T(8,128)}, f32[232,256]{1,0:T(8,128)S(1)}, u32[]{:S(2)}, u32[]{:S(2)}) collective-permute-start(f32[232,256]{1,0:T(8,128)} %get-tuple-element.23), channel_id=1, source_target_pairs={{1,0},{2,1},{3,2},{5,4},{6,5},{7,6},{9,8},{10,9},{11,10},{13,12},{... | collective-permute-start | bytes 712712 | tf_op jit(solution)/shard_map/ppermute | solution.py:515
  41.5 0.7 copy-start.3
  42.1 0.9 copy-start.4
  78.3 14.4 %all-to-all-start.1 = ((f32[64,1,384]{2,1,0:T(1,128)}), f32[64,1,384]{2,1,0:T(1,128)S(1)}, u32[]{:S(2)}, u32[]{:S(2)}) async-start(f32[64,1,384]{2,1,0:T(1,128)} %copy.23), calls=%async_computation.1 | async-start | bytes 196608 | tf_op jit(solution)/shard_map/all_to_all | solution.py:543
  92.6 1.7 copy-start

commit v3 on v2

--- a/solution.py
+++ b/solution.py
@@ -129,7 +129,8 @@
 Y_COUNTS, Y_BEGINS, Y_TOTAL = y_rows()
 
 
-def join_kernel(e_ref, l1_ref, r1_ref, l2_ref, r2_ref, sx_ref, upper_ref, lower_ref):
+def join_kernel(e_ref, l1_ref, r1_ref, l2_ref, r2_ref, order_ref, sx_ref, upper_ref, lower_ref):
+    del order_ref
     parts = ((l1_ref, 2, 10), (r1_ref, 18, 10), (l2_ref, 0, 4), (r2_ref, 26, 4))
     upper_ref[Y_TOTAL - 8 :, :] = jnp.zeros((8, CZ), F32)
     lower_ref[Y_TOTAL - 8 :, :] = jnp.zeros((8, CZ), F32)
@@ -148,15 +149,15 @@
         lower_ref[at : at + rows, :] = sx_ref[plane, 3 : 3 + rows, :]
 
 
-def join_x(own, l1, r1, l2, r2):
+def join_x(own, l1, r1, l2, r2, order):
     return pl.pallas_call(
         join_kernel,
         out_shape=(shaped(XS, 40, CZ), shaped(Y_TOTAL, CZ), shaped(Y_TOTAL, CZ)),
-        in_specs=[VMEM] * 5,
+        in_specs=[VMEM] * 6,
         out_specs=(VMEM,) * 3,
         compiler_params=PARAMS,
         name="join_x",
-    )(own, l1, r1, l2, r2)
+    )(own, l1, r1, l2, r2, order)
 
 
 def plane_rows(reach):
@@ -291,9 +292,10 @@
 LEFT = (0, 0, 0, 1, 1, 2)
 
 
-def prepare_kernel(place_ref, position_ref, moment_ref, left_ref, right_ref, face_ref):
+def prepare_kernel(place_ref, position_ref, moment_ref, left_ref, right_ref, face_ref, order_ref):
     brick, row = place_ref[0], place_ref[1]
     sub = lax.broadcasted_iota(jnp.int32, (8, QUARTER), 0)
+    order_ref[...] = jnp.zeros((8, HALF), F32)
 
     def sources(b, carry):
         node = pl.multiple_of(b * BLOCK + row * QUARTER, HALF)
@@ -327,9 +329,14 @@
 def prepare(place, position, moment):
     return pl.pallas_call(
         prepare_kernel,
-        out_shape=(shaped(BLOCK, 48, dtype=BF16), shaped(48, SRC, dtype=BF16), shaped(8, SRC)),
+        out_shape=(
+            shaped(BLOCK, 48, dtype=BF16),
+            shaped(48, SRC, dtype=BF16),
+            shaped(8, SRC),
+            shaped(8, HALF),
+        ),
         in_specs=[SMEM, VMEM, VMEM],
-        out_specs=(VMEM, VMEM, VMEM),
+        out_specs=(VMEM,) * 4,
         compiler_params=PARAMS,
         name="prepare",
     )(place, position, moment)
@@ -529,12 +536,12 @@
     base = jnp.concatenate([slot_f, zeros, cell_f], axis=1)
     cells = cell.T.reshape(2, 6, bricks).transpose(1, 0, 2).reshape(6, 2 * bricks)
     fraction = lax.dynamic_slice_in_dim(solid_fraction, brick * 1536 + row * 384, 384, 0)[None]
-    left, right, moment = prepare(place, node_position, node_moment)
+    left, right, moment, order = prepare(place, node_position, node_moment)
 
     own, flat, low, high = own_source(magnet)
     l1, r1 = shifted(flat, "brick", 1), shifted(flat, "brick", -1)
     l2, r2 = shifted(high, "brick", 2), shifted(low, "brick", -2)
-    sx, upper, lower = join_x(own, l1, r1, l2, r2)
+    sx, upper, lower = join_x(own, l1, r1, l2, r2, order)
     below, above = shifted(upper, "row", 1), shifted(lower, "row", -1)
     first, message = first_solve(place, sx, below, above, cells, base)
     message = message.reshape(rows * bricks, 3 * CAP)

time: 179 us -> 175 us (0.978)
  blocking collectives: 48.9 us -> 45.5 us
    ppermute x6, waiting for transfers between devices: 15.2 us -> 10.8 us  [shifted(): return lax.ppermute(x, axis, pairs)]
    all_to_all x1, waiting for transfers between devices: 4.55 us -> 8.64 us  [local(): lax.all_to_all(quarter, 'brick', split_axis=0, concat_axis=0, tiled=True)]
    all_to_all x1, blocking collectives: 25.5 us -> 23.1 us  [local(): lax.all_to_all(message, ('row', 'brick'), split_axis=0, concat_axis=0, ti...]
    unnamed x20 -> x18, local copies, waits for them, and re-layouts: 6.68 us -> 6.67 us
  transfers between devices with their start and end apart: 7 -> 7, of which waited for: 5 -> 4; matrix products, arithmetic and copies ran while one was open for 1% -> 2% of each run, Pallas kernels for 2% -> 2%
where the time goes in v3:
time: 175 us
  Pallas kernels  73.5 us (42%)
  blocking collectives  45.5 us (26%)
  starting transfers between devices  26 us (15%)
  waiting for transfers between devices  19.4 us (11%)
  local copies, waits for them, and re-layouts  9.09 us (5%)
    pallas_call x1, Pallas kernels, layer(): pl.pallas_call(layer_kernel, out_shape=shaped(1, 1536), in_specs=[SMEM] +...  45 us
    all_to_all x1, blocking collectives, local(): lax.all_to_all(message, ('row', 'brick'), split_axis=0, concat_axis=0, ti...  23.1 us
    ppermute x6, starting transfers between devices, shifted(): return lax.ppermute(x, axis, pairs)  20.4 us
    all_to_all x1, blocking collectives, local(): lax.all_to_all(reply, 'brick', split_axis=0, concat_axis=0, tiled=True)  13.9 us
    pallas_call x1, Pallas kernels, second_solve(): pl.pallas_call(second_kernel, out_shape=shaped(CX, CY, CZ), in_specs=[SME...  13 us
    ppermute x6, waiting for transfers between devices, shifted(): return lax.ppermute(x, axis, pairs)  10.8 us
    all_to_all x1, waiting for transfers between devices, local(): lax.all_to_all(quarter, 'brick', split_axis=0, concat_axis=0, tiled=True)  8.64 us
    all_gather x1, blocking collectives, local(): partials = lax.all_gather(partial, 'row', axis=0, tiled=True)  8.46 us
  transfers between devices with their start and end apart: 7, of which 4 were waited for; matrix products, arithmetic and copies ran while one was open for 2% of the time, Pallas kernels for 2%

profile of v3, /device:TPU:1, one launch (start us, length us, event | category | flops | bytes accessed | tf_op | source)
XLA Modules:
  0.0 174.7 jit_solution(11257133671417146389)
XLA Ops:
  0.6 1.1 copy-done.2
  1.8 0.3 own_source.1
  2.1 4.4 %collective-permute-start = (f32[340,256]{1,0:T(8,128)S(1)}, f32[340,256]{1,0:T(8,128)S(1)}, u32[]{:S(2)}, u32[]{:S(2)}) collective-permute-start(f32[340,256]{1,0:T(8,128)S(1)} %get-tuple-element.19), channel_id=1, source_target_pairs={{0,4},{4,8},{8,12},{12,16},{16,20},{20,24},{24,28},{28,32},{32,36}... | collective-permute-start | bytes 1044488 | tf_op jit(solution)/shard_map/ppermute | solution.py:522
  6.5 1.3 collective-permute-start.1
  7.8 5.5 %collective-permute-start.2 = (f32[136,256]{1,0:T(8,128)S(1)}, f32[136,256]{1,0:T(8,128)S(1)}, u32[]{:S(2)}, u32[]{:S(2)}) collective-permute-start(f32[136,256]{1,0:T(8,128)S(1)} %get-tuple-element.20), channel_id=1, source_target_pairs={{0,8},{4,12},{8,16},{12,20},{16,24},{20,28},{24,32},{28,36},{32,40... | collective-permute-start | bytes 417800 | tf_op jit(solution)/shard_map/ppermute | solution.py:522
  13.3 1.3 collective-permute-start.3
  14.6 0.7 copy.37
  15.3 0.8 copy.18
  16.2 0.8 copy.21
  17.1 1.4 copy-done.1
  18.5 4.2 %prepare.1 = (bf16[1536,48]{1,0:T(8,128)(2,1)S(1)}, bf16[48,24576]{1,0:T(8,128)(2,1)}, f32[8,24576]{1,0:T(8,128)S(1)}, f32[8,128]{1,0:T(8,128)S(1)}) custom-call(s32[4]{0:T(128)S(1)} %pad_add_fusion.place_ref, f32[3,98304]{1,0:T(4,128)S(1)} %copy-done.1, f32[3,98304]{1,0:T(4,128)} %moment_ref.1), custom_call_target="tpu_custom_call" | custom-call | tf_op jit(solution)/shard_map/prepare/pallas_call | solution.py:330
  22.7 4.0 %collective-permute-done.3.r2_ref = f32[136,256]{1,0:T(8,128)S(1)} collective-permute-done((f32[136,256]{1,0:T(8,128)S(1)}, f32[136,256]{1,0:T(8,128)S(1)}, u32[]{:S(2)}, u32[]{:S(2)}) %collective-permute-start.3) | collective-permute-done | bytes 139296 | tf_op jit(solution)/shard_map/ppermute | solution.py:522
  26.7 0.3 join_x.1
  27.0 6.0 %collective-permute-start.4 = (f32[232,256]{1,0:T(8,128)S(1)}, f32[232,256]{1,0:T(8,128)S(1)}, u32[]{:S(2)}, u32[]{:S(2)}) collective-permute-start(f32[232,256]{1,0:T(8,128)S(1)} %get-tuple-element.24), channel_id=1, source_target_pairs={{0,1},{1,2},{2,3},{4,5},{5,6},{6,7},{8,9},{9,10},{10,11},{12,13},{... | collective-permute-start | bytes 712712 | tf_op jit(solution)/shard_map/ppermute | solution.py:522
  33.0 1.9 %collective-permute-start.5 = (f32[232,256]{1,0:T(8,128)S(1)}, f32[232,256]{1,0:T(8,128)S(1)}, u32[]{:S(2)}, u32[]{:S(2)}) collective-permute-start(f32[232,256]{1,0:T(8,128)S(1)} %get-tuple-element.25), channel_id=1, source_target_pairs={{1,0},{2,1},{3,2},{5,4},{6,5},{7,6},{9,8},{10,9},{11,10},{13,12},{... | collective-permute-start | bytes 712712 | tf_op jit(solution)/shard_map/ppermute | solution.py:522
  35.1 0.9 collective-permute-done.4.below_ref
  36.0 5.9 %collective-permute-done.5.above_ref = f32[232,256]{1,0:T(8,128)S(1)} collective-permute-done((f32[232,256]{1,0:T(8,128)S(1)}, f32[232,256]{1,0:T(8,128)S(1)}, u32[]{:S(2)}, u32[]{:S(2)}) %collective-permute-start.5) | collective-permute-done | bytes 237600 | tf_op jit(solution)/shard_map/ppermute | solution.py:522
  41.9 7.2 %first_solve.1 = (f32[8,32,256]{2,1,0:T(8,128)S(1)}, f32[4,64,36]{2,1,0:T(8,128)S(1)}) custom-call(s32[4]{0:T(128)S(1)} %pad_add_fusion.place_ref, f32[30,40,256]{2,1,0:T(8,128)S(1)} %get-tuple-element.23.sx_ref, f32[232,256]{1,0:T(8,128)S(1)} %collective-permute-done.4.below_ref, f32[232,256]{1,0:T(8,128)S(1)} %collective-permute-done.5.above_ref, ...), custom_call_target="tpu_custom_call" | custom-call | tf_op jit(solution)/shard_map/first_solve/pallas_call | solution.py:244
  49.2 23.1 %all_to_all.33 = f32[256,1,36]{2,1,0:T(1,128)S(1)} all-to-all(f32[256,1,36]{2,1,0:T(1,128)S(1)} %bitcast.41), channel_id=1, replica_groups=mesh['brick'=64,'row'=4] {'row','brick'}, dimensions={0} | all-to-all | bytes 73728 | tf_op jit(solution)/shard_map/all_to_all | solution.py:548
  72.2 1.6 place_quarter.1
  73.9 0.7 copy.23
  74.6 5.6 %all-to-all-start.1 = ((f32[64,1,384]{2,1,0:T(1,128)}), f32[64,1,384]{2,1,0:T(1,128)}, u32[]{:S(2)}, u32[]{:S(2)}) async-start(f32[64,1,384]{2,1,0:T(1,128)} %copy.23), calls=%async_computation.1 | async-start | bytes 196608 | tf_op jit(solution)/shard_map/all_to_all | solution.py:550
  80.2 0.8 dynamic_slice.3
  81.0 8.6 %all-to-all-done.1 = f32[64,1,384]{2,1,0:T(1,128)} async-done(((f32[64,1,384]{2,1,0:T(1,128)}), f32[64,1,384]{2,1,0:T(1,128)}, u32[]{:S(2)}, u32[]{:S(2)}) %all-to-all-start.1) | async-done | bytes 98336 | tf_op jit(solution)/shard_map/all_to_all | solution.py:550
  89.7 0.9 copy.35
  90.6 1.0 copy-done.4
  91.6 45.0 %layer.1 = f32[1,1536]{1,0:T(1,128)S(1)} custom-call(s32[4]{0:T(128)S(1)} %pad_add_fusion.place_ref, bf16[1536,48]{1,0:T(8,128)(2,1)S(1)} %copy-done.4, bf16[48,24576]{1,0:T(8,128)(2,1)S(1)} %copy-done, f32[8,24576]{1,0:T(8,128)S(1)} %get-tuple-element.17.moment_ref, f32[64,384]{1,0:T(8,128)S(1)} %bitcast.40, f32[1,384]{1,0:T(1,128)S(1)} %broadcast_in_dim.22.fraction_ref), custom_call_target="tpu_custom_call" | custom-call | tf_op jit(solution)/shard_map/layer/pallas_call | solution.py:382
  136.5 8.5 %all-gather = f32[4,1,1536]{2,1,0:T(1,128)S(1)} all-gather(f32[1,1,1536]{2,1,0:T(1,128)S(1)} %bitcast.43), channel_id=1, replica_groups=mesh['brick'=64,'row'=4] {'row'}, dimensions={0}, use_global_device_ids=true | all-gather | bytes 30720 | tf_op jit(solution)/shard_map/all_gather | solution.py:552
  145.0 1.9 %answer.1 = f32[64,384]{1,0:T(8,128)S(1)} custom-call(s32[4]{0:T(128)S(1)} %pad_add_fusion.place_ref, f32[4,1536]{1,0:T(4,128)S(1)} %bitcast.42, f32[256,36]{1,0:T(8,128)S(1)} %bitcast.35), custom_call_target="tpu_custom_call" | custom-call | tf_op jit(solution)/shard_map/answer/pallas_call | solution.py:426
  147.0 13.9 %all_to_all.34 = f32[64,1,384]{2,1,0:T(1,128)S(1)} all-to-all(f32[64,1,384]{2,1,0:T(1,128)S(1)} %copy.24), channel_id=1, replica_groups=mesh['brick'=64,'row'=4] {'brick'}, dimensions={0} | all-to-all | bytes 196608 | tf_op jit(solution)/shard_map/all_to_all | solution.py:554
  161.1 13.0 %second_solve.1 = f32[8,32,256]{2,1,0:T(8,128)} custom-call(s32[4]{0:T(128)S(1)} %pad_add_fusion.place_ref, f32[64,384]{1,0:T(8,128)S(1)} %bitcast.37, f32[8,32,256]{2,1,0:T(8,128)S(1)} %get-tuple-element.27.first_ref), custom_call_target="tpu_custom_call" | custom-call | tf_op jit(solution)/shard_map/second_solve/pallas_call | solution.py:508
  174.0 0.7 copy.25
  (24 shorter events, 0.6 us)
Async XLA Ops:
  0.6 1.1 copy-start.2
  2.1 24.6 %collective-permute-start = (f32[340,256]{1,0:T(8,128)S(1)}, f32[340,256]{1,0:T(8,128)S(1)}, u32[]{:S(2)}, u32[]{:S(2)}) collective-permute-start(f32[340,256]{1,0:T(8,128)S(1)} %get-tuple-element.19), channel_id=1, source_target_pairs={{0,4},{4,8},{8,12},{12,16},{16,20},{20,24},{24,28},{28,32},{32,36}... | collective-permute-start | bytes 1044488 | tf_op jit(solution)/shard_map/ppermute | solution.py:522
  6.5 20.2 %collective-permute-start.1 = (f32[340,256]{1,0:T(8,128)S(1)}, f32[340,256]{1,0:T(8,128)S(1)}, u32[]{:S(2)}, u32[]{:S(2)}) collective-permute-start(f32[340,256]{1,0:T(8,128)S(1)} %get-tuple-element.19), channel_id=1, source_target_pairs={{4,0},{8,4},{12,8},{16,12},{20,16},{24,20},{28,24},{32,28},{36,32}... | collective-permute-start | bytes 1044488 | tf_op jit(solution)/shard_map/ppermute | solution.py:522
  7.8 14.9 %collective-permute-start.2 = (f32[136,256]{1,0:T(8,128)S(1)}, f32[136,256]{1,0:T(8,128)S(1)}, u32[]{:S(2)}, u32[]{:S(2)}) collective-permute-start(f32[136,256]{1,0:T(8,128)S(1)} %get-tuple-element.20), channel_id=1, source_target_pairs={{0,8},{4,12},{8,16},{12,20},{16,24},{20,28},{24,32},{28,36},{32,40... | collective-permute-start | bytes 417800 | tf_op jit(solution)/shard_map/ppermute | solution.py:522
  13.3 13.4 %collective-permute-start.3 = (f32[136,256]{1,0:T(8,128)S(1)}, f32[136,256]{1,0:T(8,128)S(1)}, u32[]{:S(2)}, u32[]{:S(2)}) collective-permute-start(f32[136,256]{1,0:T(8,128)S(1)} %get-tuple-element.21), channel_id=1, source_target_pairs={{8,0},{12,4},{16,8},{20,12},{24,16},{28,20},{32,24},{36,28},{40,32... | collective-permute-start | bytes 417800 | tf_op jit(solution)/shard_map/ppermute | solution.py:522
  17.1 1.4 copy-start.1
  18.5 16.5 %copy-start.5 = (s32[1,1,64]{2,1,0:T(1,128)S(1)}, s32[1,1,64]{2,1,0:T(1,128)}, u32[]{:S(2)}) copy-start(s32[1,1,64]{2,1,0:T(1,128)} %param.13) | copy-start | bytes 772
  22.7 12.2 %copy-start.3 = (bf16[1536,48]{1,0:T(8,128)(2,1)}, bf16[1536,48]{1,0:T(8,128)(2,1)S(1)}, u32[]{:S(2)}) copy-start(bf16[1536,48]{1,0:T(8,128)(2,1)S(1)} %get-tuple-element.15.left_ref) | copy-start | bytes 442372
  27.0 9.1 %collective-permute-start.4 = (f32[232,256]{1,0:T(8,128)S(1)}, f32[232,256]{1,0:T(8,128)S(1)}, u32[]{:S(2)}, u32[]{:S(2)}) collective-permute-start(f32[232,256]{1,0:T(8,128)S(1)} %get-tuple-element.24), channel_id=1, source_target_pairs={{0,1},{1,2},{2,3},{4,5},{5,6},{6,7},{8,9},{9,10},{10,11},{12,13},{... | collective-permute-start | bytes 712712 | tf_op jit(solution)/shard_map/ppermute | solution.py:522
  33.0 8.9 %collective-permute-start.5 = (f32[232,256]{1,0:T(8,128)S(1)}, f32[232,256]{1,0:T(8,128)S(1)}, u32[]{:S(2)}, u32[]{:S(2)}) collective-permute-start(f32[232,256]{1,0:T(8,128)S(1)} %get-tuple-element.25), channel_id=1, source_target_pairs={{1,0},{2,1},{3,2},{5,4},{6,5},{7,6},{9,8},{10,9},{11,10},{13,12},{... | collective-permute-start | bytes 712712 | tf_op jit(solution)/shard_map/ppermute | solution.py:522
  34.9 55.6 %copy-start = (bf16[48,24576]{1,0:T(8,128)(2,1)S(1)}, bf16[48,24576]{1,0:T(8,128)(2,1)}, u32[]{:S(2)}) copy-start(bf16[48,24576]{1,0:T(8,128)(2,1)} %get-tuple-element.16.right_ref) | copy-start | bytes 7077892
  74.6 15.1 %all-to-all-start.1 = ((f32[64,1,384]{2,1,0:T(1,128)}), f32[64,1,384]{2,1,0:T(1,128)}, u32[]{:S(2)}, u32[]{:S(2)}) async-start(f32[64,1,384]{2,1,0:T(1,128)} %copy.23), calls=%async_computation.1 | async-start | bytes 196608 | tf_op jit(solution)/shard_map/all_to_all | solution.py:550
  90.6 1.0 copy-start.4

commit v4 on v3

--- a/solution.py
+++ b/solution.py
@@ -292,8 +292,8 @@
 LEFT = (0, 0, 0, 1, 1, 2)
 
 
-def prepare_kernel(place_ref, position_ref, moment_ref, left_ref, right_ref, face_ref, order_ref):
-    brick, row = place_ref[0], place_ref[1]
+def prepare_kernel(place_ref, position_ref, moment_ref, right_ref, face_ref, order_ref):
+    row = place_ref[1]
     sub = lax.broadcasted_iota(jnp.int32, (8, QUARTER), 0)
     order_ref[...] = jnp.zeros((8, HALF), F32)
 
@@ -314,10 +314,27 @@
         return carry
 
     lax.fori_loop(0, SRC // QUARTER, sources, 0, unroll=2)
+
+
+def prepare(place, position, moment):
+    return pl.pallas_call(
+        prepare_kernel,
+        out_shape=(
+            shaped(48, SRC, dtype=BF16),
+            shaped(8, SRC),
+            shaped(8, HALF),
+        ),
+        in_specs=[SMEM, VMEM, VMEM],
+        out_specs=(VMEM,) * 3,
+        compiler_params=PARAMS,
+        name="prepare",
+    )(place, position, moment)
+
+
+def targets_kernel(target_ref, left_ref):
     sub = lax.broadcasted_iota(jnp.int32, (8, TILE), 0)
     for t in range(BLOCK // TILE):
-        node = pl.multiple_of(brick * BLOCK + t * TILE, HALF)
-        pos = position_ref[:, pl.ds(node, TILE)] - 4.0
+        pos = target_ref[:, t * TILE : (t + 1) * TILE] - 4.0
         norm = jnp.sum(pos * pos, axis=0, keepdims=True) + SOFTENING
         feat = jnp.where(sub == 3, norm, jnp.where(sub == 4, 1.0, 0.0))
         for i in range(3):
@@ -326,20 +343,15 @@
         left_ref[t * TILE : (t + 1) * TILE, :] = rows.T[:, :48].astype(BF16)
 
 
-def prepare(place, position, moment):
-    return pl.pallas_call(
-        prepare_kernel,
-        out_shape=(
-            shaped(BLOCK, 48, dtype=BF16),
-            shaped(48, SRC, dtype=BF16),
-            shaped(8, SRC),
-            shaped(8, HALF),
-        ),
-        in_specs=[SMEM, VMEM, VMEM],
-        out_specs=(VMEM,) * 4,
-        compiler_params=PARAMS,
-        name="prepare",
-    )(place, position, moment)
+def prepare_targets(targets):
+    return pl.pallas_call(
+        targets_kernel,
+        out_shape=shaped(BLOCK, 48, dtype=BF16),
+        in_specs=[VMEM],
+        out_specs=VMEM,
+        compiler_params=PARAMS,
+        name="prepare_targets",
+    )(targets)
 
 
 def layer_kernel(place_ref, left_ref, right_ref, moment_ref, trace_ref, fraction_ref, out_ref, acc):
@@ -536,7 +548,9 @@
     base = jnp.concatenate([slot_f, zeros, cell_f], axis=1)
     cells = cell.T.reshape(2, 6, bricks).transpose(1, 0, 2).reshape(6, 2 * bricks)
     fraction = lax.dynamic_slice_in_dim(solid_fraction, brick * 1536 + row * 384, 384, 0)[None]
-    left, right, moment, order = prepare(place, node_position, node_moment)
+    right, moment, order = prepare(place, node_position, node_moment)
+    targets = lax.dynamic_slice_in_dim(node_position, brick * BLOCK, BLOCK, 1)
+    left = prepare_targets(targets)
 
     own, flat, low, high = own_source(magnet)
     l1, r1 = shifted(flat, "brick", 1), shifted(flat, "brick", -1)

time: 175 us -> 175 us (level)
  blocking collectives: 45.5 us -> 22.4 us
  waiting for transfers between devices: 19.4 us -> 30.8 us
  starting transfers between devices: 26 us -> 36.2 us
    all_to_all x1 -> x0, blocking collectives: 23.1 us -> none  [local(): lax.all_to_all(message, ('row', 'brick'), split_axis=0, concat_axis=0, ti...]
    all_to_all x0 -> x1, waiting for transfers between devices: none -> 11.9 us  [local(): lax.all_to_all(message, ('row', 'brick'), split_axis=0, concat_axis=0, ti...]
    all_to_all x0 -> x1, starting transfers between devices: none -> 11 us  [local(): lax.all_to_all(message, ('row', 'brick'), split_axis=0, concat_axis=0, ti...]
    pallas_call x1 -> x2, Pallas kernels: 4.23 us -> 3.54 us  [the longest x1 3.35 us: prepare(): pl.pallas_call(prepare_kernel, out_shape=(shaped(48, SRC, dtype=BF16), sh...]
    unnamed x18 -> x20, local copies, waits for them, and re-layouts: 6.67 us -> 7.33 us
  transfers between devices with their start and end apart: 7 -> 8, of which waited for: 4 -> 5; matrix products, arithmetic and copies ran while one was open for 2% -> 2% of each run, Pallas kernels for 2% -> 2%
where the time goes in v4:
time: 175 us
  Pallas kernels  73.5 us (42%)
  starting transfers between devices  36.2 us (21%)
  waiting for transfers between devices  30.8 us (18%)
  blocking collectives  22.4 us (13%)
  local copies, waits for them, and re-layouts  10.5 us (6%)
    pallas_call x1, Pallas kernels, layer(): pl.pallas_call(layer_kernel, out_shape=shaped(1, 1536), in_specs=[SMEM] +...  45 us
    ppermute x6, starting transfers between devices, shifted(): return lax.ppermute(x, axis, pairs)  20.4 us
    all_to_all x1, blocking collectives, local(): lax.all_to_all(reply, 'brick', split_axis=0, concat_axis=0, tiled=True)  13.9 us
    pallas_call x1, Pallas kernels, second_solve(): pl.pallas_call(second_kernel, out_shape=shaped(CX, CY, CZ), in_specs=[SME...  13 us
    all_to_all x1, waiting for transfers between devices, local(): lax.all_to_all(message, ('row', 'brick'), split_axis=0, concat_axis=0, ti...  11.9 us
    all_to_all x1, starting transfers between devices, local(): lax.all_to_all(message, ('row', 'brick'), split_axis=0, concat_axis=0, ti...  11 us
    ppermute x6, waiting for transfers between devices, shifted(): return lax.ppermute(x, axis, pairs)  10.3 us
    all_to_all x1, waiting for transfers between devices, local(): lax.all_to_all(quarter, 'brick', split_axis=0, concat_axis=0, tiled=True)  8.62 us
  transfers between devices with their start and end apart: 8, of which 5 were waited for; matrix products, arithmetic and copies ran while one was open for 2% of the time, Pallas kernels for 2%

profile of v4, /device:TPU:1, one launch (start us, length us, event | category | flops | bytes accessed | tf_op | source)
XLA Modules:
  0.0 174.6 jit_solution(1730308858414425195)
XLA Ops:
  0.6 1.1 copy-done.5
  2.1 4.4 %collective-permute-start = (f32[340,256]{1,0:T(8,128)S(1)}, f32[340,256]{1,0:T(8,128)S(1)}, u32[]{:S(2)}, u32[]{:S(2)}) collective-permute-start(f32[340,256]{1,0:T(8,128)S(1)} %get-tuple-element.17), channel_id=1, source_target_pairs={{0,4},{4,8},{8,12},{12,16},{16,20},{20,24},{24,28},{28,32},{32,36}... | collective-permute-start | bytes 1044488 | tf_op jit(solution)/shard_map/ppermute | solution.py:534
  6.5 1.3 collective-permute-start.1
  7.8 5.5 %collective-permute-start.2 = (f32[136,256]{1,0:T(8,128)S(1)}, f32[136,256]{1,0:T(8,128)S(1)}, u32[]{:S(2)}, u32[]{:S(2)}) collective-permute-start(f32[136,256]{1,0:T(8,128)S(1)} %get-tuple-element.18), channel_id=1, source_target_pairs={{0,8},{4,12},{8,16},{12,20},{16,24},{20,28},{24,32},{28,36},{32,40... | collective-permute-start | bytes 417800 | tf_op jit(solution)/shard_map/ppermute | solution.py:534
  13.3 1.3 collective-permute-start.3
  14.6 0.8 copy.18
  15.4 0.7 copy.37
  16.1 0.8 copy.21
  17.1 1.4 copy-done.1
  18.5 1.4 copy-done.2
  19.9 3.4 %prepare.1 = (bf16[48,24576]{1,0:T(8,128)(2,1)}, f32[8,24576]{1,0:T(8,128)S(1)}, f32[8,128]{1,0:T(8,128)S(1)}) custom-call(s32[4]{0:T(128)S(1)} %pad_add_fusion.place_ref, f32[3,98304]{1,0:T(4,128)S(1)} %copy-done.1, f32[3,98304]{1,0:T(4,128)S(1)} %copy-done.2), custom_call_target="tpu_custom_call" | custom-call | tf_op jit(solution)/shard_map/prepare/pallas_call | solution.py:320
  23.2 3.5 %collective-permute-done.3.r2_ref = f32[136,256]{1,0:T(8,128)S(1)} collective-permute-done((f32[136,256]{1,0:T(8,128)S(1)}, f32[136,256]{1,0:T(8,128)S(1)}, u32[]{:S(2)}, u32[]{:S(2)}) %collective-permute-start.3) | collective-permute-done | bytes 139296 | tf_op jit(solution)/shard_map/ppermute | solution.py:534
  27.0 6.0 %collective-permute-start.4 = (f32[232,256]{1,0:T(8,128)S(1)}, f32[232,256]{1,0:T(8,128)S(1)}, u32[]{:S(2)}, u32[]{:S(2)}) collective-permute-start(f32[232,256]{1,0:T(8,128)S(1)} %get-tuple-element.22), channel_id=1, source_target_pairs={{0,1},{1,2},{2,3},{4,5},{5,6},{6,7},{8,9},{9,10},{10,11},{12,13},{... | collective-permute-start | bytes 712712 | tf_op jit(solution)/shard_map/ppermute | solution.py:534
  33.0 1.9 %collective-permute-start.5 = (f32[232,256]{1,0:T(8,128)S(1)}, f32[232,256]{1,0:T(8,128)S(1)}, u32[]{:S(2)}, u32[]{:S(2)}) collective-permute-start(f32[232,256]{1,0:T(8,128)S(1)} %get-tuple-element.23), channel_id=1, source_target_pairs={{1,0},{2,1},{3,2},{5,4},{6,5},{7,6},{9,8},{10,9},{11,10},{13,12},{... | collective-permute-start | bytes 712712 | tf_op jit(solution)/shard_map/ppermute | solution.py:534
  35.1 0.9 collective-permute-done.4.below_ref
  36.0 5.9 %collective-permute-done.5.above_ref = f32[232,256]{1,0:T(8,128)S(1)} collective-permute-done((f32[232,256]{1,0:T(8,128)S(1)}, f32[232,256]{1,0:T(8,128)S(1)}, u32[]{:S(2)}, u32[]{:S(2)}) %collective-permute-start.5) | collective-permute-done | bytes 237600 | tf_op jit(solution)/shard_map/ppermute | solution.py:534
  41.9 7.9 %first_solve.1 = (f32[8,32,256]{2,1,0:T(8,128)S(1)}, f32[4,64,36]{2,1,0:T(8,128)}) custom-call(s32[4]{0:T(128)S(1)} %pad_add_fusion.place_ref, f32[30,40,256]{2,1,0:T(8,128)S(1)} %get-tuple-element.21.sx_ref, f32[232,256]{1,0:T(8,128)S(1)} %collective-permute-done.4.below_ref, f32[232,256]{1,0:T(8,128)S(1)} %collective-permute-done.5.above_ref, ...), custom_call_target="tpu_custom_call" | custom-call | tf_op jit(solution)/shard_map/first_solve/pallas_call | solution.py:244
  49.9 11.0 %all-to-all-start = ((f32[256,1,36]{2,1,0:T(1,128)}), f32[256,1,36]{2,1,0:T(1,128)S(1)}, u32[]{:S(2)}, u32[]{:S(2)}) async-start(f32[256,1,36]{2,1,0:T(1,128)} %bitcast.9), calls=%async_computation | async-start | bytes 262144 | tf_op jit(solution)/shard_map/all_to_all | solution.py:562
  60.9 0.8 dynamic_slice.7
  61.7 11.9 %all-to-all-done = f32[256,1,36]{2,1,0:T(1,128)S(1)} async-done(((f32[256,1,36]{2,1,0:T(1,128)}), f32[256,1,36]{2,1,0:T(1,128)S(1)}, u32[]{:S(2)}, u32[]{:S(2)}) %all-to-all-start) | async-done | bytes 36896 | tf_op jit(solution)/shard_map/all_to_all | solution.py:562
  73.6 1.6 place_quarter.1
  75.2 0.7 copy.23
  75.9 4.8 %all-to-all-start.1 = ((f32[64,1,384]{2,1,0:T(1,128)}), f32[64,1,384]{2,1,0:T(1,128)S(1)}, u32[]{:S(2)}, u32[]{:S(2)}) async-start(f32[64,1,384]{2,1,0:T(1,128)} %copy.23), calls=%async_computation.1 | async-start | bytes 196608 | tf_op jit(solution)/shard_map/all_to_all | solution.py:564
  80.8 0.7 constant_dynamic-slice_fusion.target_ref
  81.7 8.6 %all-to-all-done.1 = f32[64,1,384]{2,1,0:T(1,128)S(1)} async-done(((f32[64,1,384]{2,1,0:T(1,128)}), f32[64,1,384]{2,1,0:T(1,128)S(1)}, u32[]{:S(2)}, u32[]{:S(2)}) %all-to-all-start.1) | async-done | bytes 98336 | tf_op jit(solution)/shard_map/all_to_all | solution.py:564
  90.3 1.1 copy-done.4
  91.5 45.0 %layer.1 = f32[1,1536]{1,0:T(1,128)S(1)} custom-call(s32[4]{0:T(128)S(1)} %pad_add_fusion.place_ref, bf16[1536,48]{1,0:T(8,128)(2,1)S(1)} %prepare_targets.1.left_ref, bf16[48,24576]{1,0:T(8,128)(2,1)S(1)} %copy-done, f32[8,24576]{1,0:T(8,128)S(1)} %copy-done.4, f32[64,384]{1,0:T(8,128)S(1)} %bitcast.40, f32[1,384]{1,0:T(1,128)S(1)} %broadcast_in_dim.22.fraction_ref), custom_call_target="tpu_custom_call" | custom-call | tf_op jit(solution)/shard_map/layer/pallas_call | solution.py:394
  136.4 8.5 %all-gather = f32[4,1,1536]{2,1,0:T(1,128)S(1)} all-gather(f32[1,1,1536]{2,1,0:T(1,128)S(1)} %bitcast.42), channel_id=1, replica_groups=mesh['brick'=64,'row'=4] {'row'}, dimensions={0}, use_global_device_ids=true | all-gather | bytes 30720 | tf_op jit(solution)/shard_map/all_gather | solution.py:566
  144.9 1.9 %answer.1 = f32[64,384]{1,0:T(8,128)S(1)} custom-call(s32[4]{0:T(128)S(1)} %pad_add_fusion.place_ref, f32[4,1536]{1,0:T(4,128)S(1)} %bitcast.41, f32[256,36]{1,0:T(8,128)S(1)} %bitcast.35), custom_call_target="tpu_custom_call" | custom-call | tf_op jit(solution)/shard_map/answer/pallas_call | solution.py:438
  146.9 13.9 %all_to_all.33 = f32[64,1,384]{2,1,0:T(1,128)S(1)} all-to-all(f32[64,1,384]{2,1,0:T(1,128)S(1)} %copy.24), channel_id=1, replica_groups=mesh['brick'=64,'row'=4] {'brick'}, dimensions={0} | all-to-all | bytes 196608 | tf_op jit(solution)/shard_map/all_to_all | solution.py:568
  160.9 13.0 %second_solve.1 = f32[8,32,256]{2,1,0:T(8,128)} custom-call(s32[4]{0:T(128)S(1)} %pad_add_fusion.place_ref, f32[64,384]{1,0:T(8,128)S(1)} %bitcast.37, f32[8,32,256]{2,1,0:T(8,128)S(1)} %get-tuple-element.25.first_ref), custom_call_target="tpu_custom_call" | custom-call | tf_op jit(solution)/shard_map/second_solve/pallas_call | solution.py:520
  173.9 0.7 copy.25
  (29 shorter events, 1.3 us)
Async XLA Ops:
  0.6 1.1 copy-start.5
  2.1 24.6 %collective-permute-start = (f32[340,256]{1,0:T(8,128)S(1)}, f32[340,256]{1,0:T(8,128)S(1)}, u32[]{:S(2)}, u32[]{:S(2)}) collective-permute-start(f32[340,256]{1,0:T(8,128)S(1)} %get-tuple-element.17), channel_id=1, source_target_pairs={{0,4},{4,8},{8,12},{12,16},{16,20},{20,24},{24,28},{28,32},{32,36}... | collective-permute-start | bytes 1044488 | tf_op jit(solution)/shard_map/ppermute | solution.py:534
  6.5 20.2 %collective-permute-start.1 = (f32[340,256]{1,0:T(8,128)S(1)}, f32[340,256]{1,0:T(8,128)S(1)}, u32[]{:S(2)}, u32[]{:S(2)}) collective-permute-start(f32[340,256]{1,0:T(8,128)S(1)} %get-tuple-element.17), channel_id=1, source_target_pairs={{4,0},{8,4},{12,8},{16,12},{20,16},{24,20},{28,24},{32,28},{36,32}... | collective-permute-start | bytes 1044488 | tf_op jit(solution)/shard_map/ppermute | solution.py:534
  7.8 15.4 %collective-permute-start.2 = (f32[136,256]{1,0:T(8,128)S(1)}, f32[136,256]{1,0:T(8,128)S(1)}, u32[]{:S(2)}, u32[]{:S(2)}) collective-permute-start(f32[136,256]{1,0:T(8,128)S(1)} %get-tuple-element.18), channel_id=1, source_target_pairs={{0,8},{4,12},{8,16},{12,20},{16,24},{20,28},{24,32},{28,36},{32,40... | collective-permute-start | bytes 417800 | tf_op jit(solution)/shard_map/ppermute | solution.py:534
  13.3 13.4 %collective-permute-start.3 = (f32[136,256]{1,0:T(8,128)S(1)}, f32[136,256]{1,0:T(8,128)S(1)}, u32[]{:S(2)}, u32[]{:S(2)}) collective-permute-start(f32[136,256]{1,0:T(8,128)S(1)} %get-tuple-element.19), channel_id=1, source_target_pairs={{8,0},{12,4},{16,8},{20,12},{24,16},{28,20},{32,24},{36,28},{40,32... | collective-permute-start | bytes 417800 | tf_op jit(solution)/shard_map/ppermute | solution.py:534
  17.1 1.4 copy-start.1
  18.5 1.4 copy-start.2
  19.9 15.0 %copy-start.6 = (s32[1,1,64]{2,1,0:T(1,128)S(1)}, s32[1,1,64]{2,1,0:T(1,128)}, u32[]{:S(2)}) copy-start(s32[1,1,64]{2,1,0:T(1,128)} %param.13) | copy-start | bytes 772
  23.2 26.6 %copy-start.3 = (f32[8,24576]{1,0:T(8,128)}, f32[8,24576]{1,0:T(8,128)S(1)}, u32[]{:S(2)}) copy-start(f32[8,24576]{1,0:T(8,128)S(1)} %get-tuple-element.15.moment_ref) | copy-start | bytes 2359300
  27.0 9.1 %collective-permute-start.4 = (f32[232,256]{1,0:T(8,128)S(1)}, f32[232,256]{1,0:T(8,128)S(1)}, u32[]{:S(2)}, u32[]{:S(2)}) collective-permute-start(f32[232,256]{1,0:T(8,128)S(1)} %get-tuple-element.22), channel_id=1, source_target_pairs={{0,1},{1,2},{2,3},{4,5},{5,6},{6,7},{8,9},{9,10},{10,11},{12,13},{... | collective-permute-start | bytes 712712 | tf_op jit(solution)/shard_map/ppermute | solution.py:534
  33.0 8.9 %collective-permute-start.5 = (f32[232,256]{1,0:T(8,128)S(1)}, f32[232,256]{1,0:T(8,128)S(1)}, u32[]{:S(2)}, u32[]{:S(2)}) collective-permute-start(f32[232,256]{1,0:T(8,128)S(1)} %get-tuple-element.23), channel_id=1, source_target_pairs={{1,0},{2,1},{3,2},{5,4},{6,5},{7,6},{9,8},{10,9},{11,10},{13,12},{... | collective-permute-start | bytes 712712 | tf_op jit(solution)/shard_map/ppermute | solution.py:534
  41.9 48.4 %copy-start = (bf16[48,24576]{1,0:T(8,128)(2,1)S(1)}, bf16[48,24576]{1,0:T(8,128)(2,1)}, u32[]{:S(2)}) copy-start(bf16[48,24576]{1,0:T(8,128)(2,1)} %get-tuple-element.14.right_ref) | copy-start | bytes 7077892
  49.9 23.7 %all-to-all-start = ((f32[256,1,36]{2,1,0:T(1,128)}), f32[256,1,36]{2,1,0:T(1,128)S(1)}, u32[]{:S(2)}, u32[]{:S(2)}) async-start(f32[256,1,36]{2,1,0:T(1,128)} %bitcast.9), calls=%async_computation | async-start | bytes 262144 | tf_op jit(solution)/shard_map/all_to_all | solution.py:562
  75.9 14.4 %all-to-all-start.1 = ((f32[64,1,384]{2,1,0:T(1,128)}), f32[64,1,384]{2,1,0:T(1,128)S(1)}, u32[]{:S(2)}, u32[]{:S(2)}) async-start(f32[64,1,384]{2,1,0:T(1,128)} %copy.23), calls=%async_computation.1 | async-start | bytes 196608 | tf_op jit(solution)/shard_map/all_to_all | solution.py:564
  90.3 1.1 copy-start.4

commit v5 on v4

--- a/solution.py
+++ b/solution.py
@@ -262,13 +262,13 @@
         trace = got[:, CAP + i : CAP + i + 1]
         acc = acc + jnp.where(at == slot, trace, 0.0)
     total = jnp.sum(acc, axis=0, keepdims=True)
-    out_ref[...] = jnp.broadcast_to(total, (64, 384))
+    out_ref[...] = jnp.broadcast_to(total[None], (64, 1, 384))
 
 
 def place_quarter(place, got):
     return pl.pallas_call(
         place_kernel,
-        out_shape=shaped(64, 384),
+        out_shape=shaped(64, 1, 384),
         in_specs=[SMEM, VMEM],
         out_specs=VMEM,
         compiler_params=PARAMS,
@@ -562,6 +562,7 @@
     got = lax.all_to_all(message, ("row", "brick"), split_axis=0, concat_axis=0, tiled=True)
     quarter = place_quarter(place, got)
     traces = lax.all_to_all(quarter, "brick", split_axis=0, concat_axis=0, tiled=True)
+    traces = traces.reshape(bricks, QUARTER)
     partial = layer(place, left, right, moment, traces, fraction)
     partials = lax.all_gather(partial, "row", axis=0, tiled=True)
     reply = answer(place, partials, got)

time: 175 us -> 175 us (level)
  no operation moved by 1% of the time
where the time goes in v5:
time: 175 us; the launch traced here: 174 us
  Pallas kernels  74.2 us (42%)
  starting transfers between devices  36.2 us (21%)
  waiting for transfers between devices  30.8 us (18%)
  blocking collectives  22.3 us (13%)
  local copies, waits for them, and re-layouts  9.75 us (6%)
    pallas_call x1, Pallas kernels, layer(): pl.pallas_call(layer_kernel, out_shape=shaped(1, 1536), in_specs=[SMEM] +...  45 us
    ppermute x6, starting transfers between devices, shifted(): return lax.ppermute(x, axis, pairs)  20.4 us
    all_to_all x1, blocking collectives, local(): lax.all_to_all(reply, 'brick', split_axis=0, concat_axis=0, tiled=True)  13.8 us
    pallas_call x1, Pallas kernels, second_solve(): pl.pallas_call(second_kernel, out_shape=shaped(CX, CY, CZ), in_specs=[SME...  13 us
    all_to_all x1, waiting for transfers between devices, local(): lax.all_to_all(message, ('row', 'brick'), split_axis=0, concat_axis=0, ti...  11.9 us
    all_to_all x1, starting transfers between devices, local(): lax.all_to_all(message, ('row', 'brick'), split_axis=0, concat_axis=0, ti...  11 us
    ppermute x6, waiting for transfers between devices, shifted(): return lax.ppermute(x, axis, pairs)  10.3 us
    all_to_all x1, waiting for transfers between devices, local(): lax.all_to_all(quarter, 'brick', split_axis=0, concat_axis=0, tiled=True)  8.62 us
  transfers between devices with their start and end apart: 8, of which 5 were waited for; matrix products, arithmetic and copies ran while one was open for 2% of the time, Pallas kernels for 2%

profile of v5, /device:TPU:1, one launch (start us, length us, event | category | flops | bytes accessed | tf_op | source)
XLA Modules:
  0.0 174.4 jit_solution(5286175765421725069)
XLA Ops:
  0.6 1.1 copy-done.5
  1.8 0.3 own_source.1
  2.1 4.4 %collective-permute-start = (f32[340,256]{1,0:T(8,128)S(1)}, f32[340,256]{1,0:T(8,128)S(1)}, u32[]{:S(2)}, u32[]{:S(2)}) collective-permute-start(f32[340,256]{1,0:T(8,128)S(1)} %get-tuple-element.17), channel_id=1, source_target_pairs={{0,4},{4,8},{8,12},{12,16},{16,20},{20,24},{24,28},{28,32},{32,36}... | collective-permute-start | bytes 1044488 | tf_op jit(solution)/shard_map/ppermute | solution.py:534
  6.5 1.3 collective-permute-start.1
  7.8 5.5 %collective-permute-start.2 = (f32[136,256]{1,0:T(8,128)S(1)}, f32[136,256]{1,0:T(8,128)S(1)}, u32[]{:S(2)}, u32[]{:S(2)}) collective-permute-start(f32[136,256]{1,0:T(8,128)S(1)} %get-tuple-element.18), channel_id=1, source_target_pairs={{0,8},{4,12},{8,16},{12,20},{16,24},{20,28},{24,32},{28,36},{32,40... | collective-permute-start | bytes 417800 | tf_op jit(solution)/shard_map/ppermute | solution.py:534
  13.3 1.3 collective-permute-start.3
  14.6 0.8 copy.20
  15.4 0.7 copy.38
  16.1 0.8 copy.23
  17.1 1.4 copy-done.1
  18.5 1.4 copy-done.2
  19.9 3.4 %prepare.1 = (bf16[48,24576]{1,0:T(8,128)(2,1)}, f32[8,24576]{1,0:T(8,128)S(1)}, f32[8,128]{1,0:T(8,128)S(1)}) custom-call(s32[4]{0:T(128)S(1)} %pad_add_fusion.place_ref, f32[3,98304]{1,0:T(4,128)S(1)} %copy-done.1, f32[3,98304]{1,0:T(4,128)S(1)} %copy-done.2), custom_call_target="tpu_custom_call" | custom-call | tf_op jit(solution)/shard_map/prepare/pallas_call | solution.py:320
  23.2 3.5 %collective-permute-done.3.r2_ref = f32[136,256]{1,0:T(8,128)S(1)} collective-permute-done((f32[136,256]{1,0:T(8,128)S(1)}, f32[136,256]{1,0:T(8,128)S(1)}, u32[]{:S(2)}, u32[]{:S(2)}) %collective-permute-start.3) | collective-permute-done | bytes 139296 | tf_op jit(solution)/shard_map/ppermute | solution.py:534
  27.0 6.0 %collective-permute-start.4 = (f32[232,256]{1,0:T(8,128)S(1)}, f32[232,256]{1,0:T(8,128)S(1)}, u32[]{:S(2)}, u32[]{:S(2)}) collective-permute-start(f32[232,256]{1,0:T(8,128)S(1)} %get-tuple-element.22), channel_id=1, source_target_pairs={{0,1},{1,2},{2,3},{4,5},{5,6},{6,7},{8,9},{9,10},{10,11},{12,13},{... | collective-permute-start | bytes 712712 | tf_op jit(solution)/shard_map/ppermute | solution.py:534
  33.0 1.9 %collective-permute-start.5 = (f32[232,256]{1,0:T(8,128)S(1)}, f32[232,256]{1,0:T(8,128)S(1)}, u32[]{:S(2)}, u32[]{:S(2)}) collective-permute-start(f32[232,256]{1,0:T(8,128)S(1)} %get-tuple-element.23), channel_id=1, source_target_pairs={{1,0},{2,1},{3,2},{5,4},{6,5},{7,6},{9,8},{10,9},{11,10},{13,12},{... | collective-permute-start | bytes 712712 | tf_op jit(solution)/shard_map/ppermute | solution.py:534
  35.1 0.9 collective-permute-done.4.below_ref
  36.0 5.9 %collective-permute-done.5.above_ref = f32[232,256]{1,0:T(8,128)S(1)} collective-permute-done((f32[232,256]{1,0:T(8,128)S(1)}, f32[232,256]{1,0:T(8,128)S(1)}, u32[]{:S(2)}, u32[]{:S(2)}) %collective-permute-start.5) | collective-permute-done | bytes 237600 | tf_op jit(solution)/shard_map/ppermute | solution.py:534
  41.9 7.9 %first_solve.1 = (f32[8,32,256]{2,1,0:T(8,128)S(1)}, f32[4,64,36]{2,1,0:T(8,128)}) custom-call(s32[4]{0:T(128)S(1)} %pad_add_fusion.place_ref, f32[30,40,256]{2,1,0:T(8,128)S(1)} %get-tuple-element.21.sx_ref, f32[232,256]{1,0:T(8,128)S(1)} %collective-permute-done.4.below_ref, f32[232,256]{1,0:T(8,128)S(1)} %collective-permute-done.5.above_ref, ...), custom_call_target="tpu_custom_call" | custom-call | tf_op jit(solution)/shard_map/first_solve/pallas_call | solution.py:244
  49.8 11.0 %all-to-all-start = ((f32[256,1,36]{2,1,0:T(1,128)}), f32[256,1,36]{2,1,0:T(1,128)S(1)}, u32[]{:S(2)}, u32[]{:S(2)}) async-start(f32[256,1,36]{2,1,0:T(1,128)} %bitcast.9), calls=%async_computation | async-start | bytes 262144 | tf_op jit(solution)/shard_map/all_to_all | solution.py:562
  60.9 0.8 dynamic_slice.7
  61.6 11.9 %all-to-all-done = f32[256,1,36]{2,1,0:T(1,128)S(1)} async-done(((f32[256,1,36]{2,1,0:T(1,128)}), f32[256,1,36]{2,1,0:T(1,128)S(1)}, u32[]{:S(2)}, u32[]{:S(2)}) %all-to-all-start) | async-done | bytes 36896 | tf_op jit(solution)/shard_map/all_to_all | solution.py:562
  73.6 2.3 %place_quarter.1 = f32[64,1,384]{2,1,0:T(1,128)} custom-call(s32[4]{0:T(128)S(1)} %pad_add_fusion.place_ref, f32[256,36]{1,0:T(8,128)S(1)} %bitcast.33), custom_call_target="tpu_custom_call" | custom-call | tf_op jit(solution)/shard_map/place_quarter/pallas_call | solution.py:269
  75.8 4.8 %all-to-all-start.1 = ((f32[64,1,384]{2,1,0:T(1,128)}), f32[64,1,384]{2,1,0:T(1,128)S(1)}, u32[]{:S(2)}, u32[]{:S(2)}) async-start(f32[64,1,384]{2,1,0:T(1,128)} %place_quarter.1), calls=%async_computation.1 | async-start | bytes 196608 | tf_op jit(solution)/shard_map/all_to_all | solution.py:564
  80.6 0.7 constant_dynamic-slice_fusion.target_ref
  81.6 8.6 %all-to-all-done.1 = f32[64,1,384]{2,1,0:T(1,128)S(1)} async-done(((f32[64,1,384]{2,1,0:T(1,128)}), f32[64,1,384]{2,1,0:T(1,128)S(1)}, u32[]{:S(2)}, u32[]{:S(2)}) %all-to-all-start.1) | async-done | bytes 98336 | tf_op jit(solution)/shard_map/all_to_all | solution.py:564
  90.2 1.1 copy-done.4
  91.3 45.0 %layer.1 = f32[1,1536]{1,0:T(1,128)S(1)} custom-call(s32[4]{0:T(128)S(1)} %pad_add_fusion.place_ref, bf16[1536,48]{1,0:T(8,128)(2,1)S(1)} %prepare_targets.1.left_ref, bf16[48,24576]{1,0:T(8,128)(2,1)S(1)} %copy-done, f32[8,24576]{1,0:T(8,128)S(1)} %copy-done.4, f32[64,384]{1,0:T(8,128)S(1)} %bitcast.38, f32[1,384]{1,0:T(1,128)S(1)} %broadcast_in_dim.22.fraction_ref), custom_call_target="tpu_custom_call" | custom-call | tf_op jit(solution)/shard_map/layer/pallas_call | solution.py:394
  136.4 8.4 %all-gather = f32[4,1,1536]{2,1,0:T(1,128)S(1)} all-gather(f32[1,1,1536]{2,1,0:T(1,128)S(1)} %bitcast.40), channel_id=1, replica_groups=mesh['brick'=64,'row'=4] {'row'}, dimensions={0}, use_global_device_ids=true | all-gather | bytes 30720 | tf_op jit(solution)/shard_map/all_gather | solution.py:567
  144.8 1.9 %answer.1 = f32[64,384]{1,0:T(8,128)S(1)} custom-call(s32[4]{0:T(128)S(1)} %pad_add_fusion.place_ref, f32[4,1536]{1,0:T(4,128)S(1)} %bitcast.39, f32[256,36]{1,0:T(8,128)S(1)} %bitcast.34), custom_call_target="tpu_custom_call" | custom-call | tf_op jit(solution)/shard_map/answer/pallas_call | solution.py:438
  146.8 13.8 %all_to_all.27 = f32[64,1,384]{2,1,0:T(1,128)S(1)} all-to-all(f32[64,1,384]{2,1,0:T(1,128)S(1)} %copy.25), channel_id=1, replica_groups=mesh['brick'=64,'row'=4] {'brick'}, dimensions={0} | all-to-all | bytes 196608 | tf_op jit(solution)/shard_map/all_to_all | solution.py:569
  160.8 13.0 %second_solve.1 = f32[8,32,256]{2,1,0:T(8,128)} custom-call(s32[4]{0:T(128)S(1)} %pad_add_fusion.place_ref, f32[64,384]{1,0:T(8,128)S(1)} %bitcast.36, f32[8,32,256]{2,1,0:T(8,128)S(1)} %get-tuple-element.25.first_ref), custom_call_target="tpu_custom_call" | custom-call | tf_op jit(solution)/shard_map/second_solve/pallas_call | solution.py:520
  173.7 0.7 copy.26
  (28 shorter events, 1.0 us)
Async XLA Ops:
  0.6 1.1 copy-start.5
  2.1 24.6 %collective-permute-start = (f32[340,256]{1,0:T(8,128)S(1)}, f32[340,256]{1,0:T(8,128)S(1)}, u32[]{:S(2)}, u32[]{:S(2)}) collective-permute-start(f32[340,256]{1,0:T(8,128)S(1)} %get-tuple-element.17), channel_id=1, source_target_pairs={{0,4},{4,8},{8,12},{12,16},{16,20},{20,24},{24,28},{28,32},{32,36}... | collective-permute-start | bytes 1044488 | tf_op jit(solution)/shard_map/ppermute | solution.py:534
  6.5 20.2 %collective-permute-start.1 = (f32[340,256]{1,0:T(8,128)S(1)}, f32[340,256]{1,0:T(8,128)S(1)}, u32[]{:S(2)}, u32[]{:S(2)}) collective-permute-start(f32[340,256]{1,0:T(8,128)S(1)} %get-tuple-element.17), channel_id=1, source_target_pairs={{4,0},{8,4},{12,8},{16,12},{20,16},{24,20},{28,24},{32,28},{36,32}... | collective-permute-start | bytes 1044488 | tf_op jit(solution)/shard_map/ppermute | solution.py:534
  7.8 15.4 %collective-permute-start.2 = (f32[136,256]{1,0:T(8,128)S(1)}, f32[136,256]{1,0:T(8,128)S(1)}, u32[]{:S(2)}, u32[]{:S(2)}) collective-permute-start(f32[136,256]{1,0:T(8,128)S(1)} %get-tuple-element.18), channel_id=1, source_target_pairs={{0,8},{4,12},{8,16},{12,20},{16,24},{20,28},{24,32},{28,36},{32,40... | collective-permute-start | bytes 417800 | tf_op jit(solution)/shard_map/ppermute | solution.py:534
  13.3 13.4 %collective-permute-start.3 = (f32[136,256]{1,0:T(8,128)S(1)}, f32[136,256]{1,0:T(8,128)S(1)}, u32[]{:S(2)}, u32[]{:S(2)}) collective-permute-start(f32[136,256]{1,0:T(8,128)S(1)} %get-tuple-element.19), channel_id=1, source_target_pairs={{8,0},{12,4},{16,8},{20,12},{24,16},{28,20},{32,24},{36,28},{40,32... | collective-permute-start | bytes 417800 | tf_op jit(solution)/shard_map/ppermute | solution.py:534
  17.1 1.4 copy-start.1
  18.5 1.4 copy-start.2
  19.9 15.0 %copy-start.6 = (s32[1,1,64]{2,1,0:T(1,128)S(1)}, s32[1,1,64]{2,1,0:T(1,128)}, u32[]{:S(2)}) copy-start(s32[1,1,64]{2,1,0:T(1,128)} %param.13) | copy-start | bytes 772
  23.2 26.6 %copy-start.3 = (f32[8,24576]{1,0:T(8,128)}, f32[8,24576]{1,0:T(8,128)S(1)}, u32[]{:S(2)}) copy-start(f32[8,24576]{1,0:T(8,128)S(1)} %get-tuple-element.15.moment_ref) | copy-start | bytes 2359300
  27.0 9.1 %collective-permute-start.4 = (f32[232,256]{1,0:T(8,128)S(1)}, f32[232,256]{1,0:T(8,128)S(1)}, u32[]{:S(2)}, u32[]{:S(2)}) collective-permute-start(f32[232,256]{1,0:T(8,128)S(1)} %get-tuple-element.22), channel_id=1, source_target_pairs={{0,1},{1,2},{2,3},{4,5},{5,6},{6,7},{8,9},{9,10},{10,11},{12,13},{... | collective-permute-start | bytes 712712 | tf_op jit(solution)/shard_map/ppermute | solution.py:534
  33.0 8.9 %collective-permute-start.5 = (f32[232,256]{1,0:T(8,128)S(1)}, f32[232,256]{1,0:T(8,128)S(1)}, u32[]{:S(2)}, u32[]{:S(2)}) collective-permute-start(f32[232,256]{1,0:T(8,128)S(1)} %get-tuple-element.23), channel_id=1, source_target_pairs={{1,0},{2,1},{3,2},{5,4},{6,5},{7,6},{9,8},{10,9},{11,10},{13,12},{... | collective-permute-start | bytes 712712 | tf_op jit(solution)/shard_map/ppermute | solution.py:534
  35.1 55.1 %copy-start = (bf16[48,24576]{1,0:T(8,128)(2,1)S(1)}, bf16[48,24576]{1,0:T(8,128)(2,1)}, u32[]{:S(2)}) copy-start(bf16[48,24576]{1,0:T(8,128)(2,1)} %get-tuple-element.14.right_ref) | copy-start | bytes 7077892
  49.8 23.7 %all-to-all-start = ((f32[256,1,36]{2,1,0:T(1,128)}), f32[256,1,36]{2,1,0:T(1,128)S(1)}, u32[]{:S(2)}, u32[]{:S(2)}) async-start(f32[256,1,36]{2,1,0:T(1,128)} %bitcast.9), calls=%async_computation | async-start | bytes 262144 | tf_op jit(solution)/shard_map/all_to_all | solution.py:562
  75.8 14.4 %all-to-all-start.1 = ((f32[64,1,384]{2,1,0:T(1,128)}), f32[64,1,384]{2,1,0:T(1,128)S(1)}, u32[]{:S(2)}, u32[]{:S(2)}) async-start(f32[64,1,384]{2,1,0:T(1,128)} %place_quarter.1), calls=%async_computation.1 | async-start | bytes 196608 | tf_op jit(solution)/shard_map/all_to_all | solution.py:564
  90.2 1.1 copy-start.4

commit v6 on v5

--- a/solution.py
+++ b/solution.py
@@ -380,7 +380,7 @@
             acc[rows, :] = total
         return carry
 
-    lax.fori_loop(0, SRC // CHUNK, chunk, 0)
+    lax.fori_loop(0, SRC // CHUNK, chunk, 0, unroll=2)
     for t in range(1536 // TILE):
         turned = acc[t * TILE : (t + 1) * TILE, :].T
         total = jnp.sum(turned, axis=0, keepdims=True)

time: 175 us -> 173 us (0.989)
  Pallas kernels: 74.2 us -> 71.8 us
    pallas_call x1, Pallas kernels: 45 us -> 42.6 us  [layer(): pl.pallas_call(layer_kernel, out_shape=shaped(1, 1536), in_specs=[SMEM] +...]
where the time goes in v6:
time: 173 us; the launch traced here: 172 us
  Pallas kernels  71.8 us (42%)
  starting transfers between devices  36.2 us (21%)
  waiting for transfers between devices  30.8 us (18%)
  blocking collectives  22.3 us (13%)
  local copies, waits for them, and re-layouts  9.75 us (6%)
    pallas_call x1, Pallas kernels, layer(): pl.pallas_call(layer_kernel, out_shape=shaped(1, 1536), in_specs=[SMEM] +...  42.6 us
    ppermute x6, starting transfers between devices, shifted(): return lax.ppermute(x, axis, pairs)  20.4 us
    all_to_all x1, blocking collectives, local(): lax.all_to_all(reply, 'brick', split_axis=0, concat_axis=0, tiled=True)  13.8 us
    pallas_call x1, Pallas kernels, second_solve(): pl.pallas_call(second_kernel, out_shape=shaped(CX, CY, CZ), in_specs=[SME...  13 us
    all_to_all x1, waiting for transfers between devices, local(): lax.all_to_all(message, ('row', 'brick'), split_axis=0, concat_axis=0, ti...  11.9 us
    all_to_all x1, starting transfers between devices, local(): lax.all_to_all(message, ('row', 'brick'), split_axis=0, concat_axis=0, ti...  11 us
    ppermute x6, waiting for transfers between devices, shifted(): return lax.ppermute(x, axis, pairs)  10.3 us
    all_to_all x1, waiting for transfers between devices, local(): lax.all_to_all(quarter, 'brick', split_axis=0, concat_axis=0, tiled=True)  8.62 us
  transfers between devices with their start and end apart: 8, of which 5 were waited for; matrix products, arithmetic and copies ran while one was open for 2% of the time, Pallas kernels for 2%

profile of v6, /device:TPU:1, one launch (start us, length us, event | category | flops | bytes accessed | tf_op | source)
XLA Modules:
  0.0 172.0 jit_solution(12778851673431770933)
XLA Ops:
  0.6 1.1 copy-done.5
  1.8 0.3 own_source.1
  2.1 4.4 %collective-permute-start = (f32[340,256]{1,0:T(8,128)S(1)}, f32[340,256]{1,0:T(8,128)S(1)}, u32[]{:S(2)}, u32[]{:S(2)}) collective-permute-start(f32[340,256]{1,0:T(8,128)S(1)} %get-tuple-element.17), channel_id=1, source_target_pairs={{0,4},{4,8},{8,12},{12,16},{16,20},{20,24},{24,28},{28,32},{32,36}... | collective-permute-start | bytes 1044488 | tf_op jit(solution)/shard_map/ppermute | solution.py:534
  6.5 1.3 collective-permute-start.1
  7.8 5.5 %collective-permute-start.2 = (f32[136,256]{1,0:T(8,128)S(1)}, f32[136,256]{1,0:T(8,128)S(1)}, u32[]{:S(2)}, u32[]{:S(2)}) collective-permute-start(f32[136,256]{1,0:T(8,128)S(1)} %get-tuple-element.18), channel_id=1, source_target_pairs={{0,8},{4,12},{8,16},{12,20},{16,24},{20,28},{24,32},{28,36},{32,40... | collective-permute-start | bytes 417800 | tf_op jit(solution)/shard_map/ppermute | solution.py:534
  13.3 1.3 collective-permute-start.3
  14.6 0.8 copy.20
  15.4 0.7 copy.38
  16.1 0.8 copy.23
  17.1 1.4 copy-done.1
  18.5 1.4 copy-done.2
  19.9 3.4 %prepare.1 = (bf16[48,24576]{1,0:T(8,128)(2,1)}, f32[8,24576]{1,0:T(8,128)S(1)}, f32[8,128]{1,0:T(8,128)S(1)}) custom-call(s32[4]{0:T(128)S(1)} %pad_add_fusion.place_ref, f32[3,98304]{1,0:T(4,128)S(1)} %copy-done.1, f32[3,98304]{1,0:T(4,128)S(1)} %copy-done.2), custom_call_target="tpu_custom_call" | custom-call | tf_op jit(solution)/shard_map/prepare/pallas_call | solution.py:320
  23.2 3.5 %collective-permute-done.3.r2_ref = f32[136,256]{1,0:T(8,128)S(1)} collective-permute-done((f32[136,256]{1,0:T(8,128)S(1)}, f32[136,256]{1,0:T(8,128)S(1)}, u32[]{:S(2)}, u32[]{:S(2)}) %collective-permute-start.3) | collective-permute-done | bytes 139296 | tf_op jit(solution)/shard_map/ppermute | solution.py:534
  27.0 6.0 %collective-permute-start.4 = (f32[232,256]{1,0:T(8,128)S(1)}, f32[232,256]{1,0:T(8,128)S(1)}, u32[]{:S(2)}, u32[]{:S(2)}) collective-permute-start(f32[232,256]{1,0:T(8,128)S(1)} %get-tuple-element.22), channel_id=1, source_target_pairs={{0,1},{1,2},{2,3},{4,5},{5,6},{6,7},{8,9},{9,10},{10,11},{12,13},{... | collective-permute-start | bytes 712712 | tf_op jit(solution)/shard_map/ppermute | solution.py:534
  33.0 1.9 %collective-permute-start.5 = (f32[232,256]{1,0:T(8,128)S(1)}, f32[232,256]{1,0:T(8,128)S(1)}, u32[]{:S(2)}, u32[]{:S(2)}) collective-permute-start(f32[232,256]{1,0:T(8,128)S(1)} %get-tuple-element.23), channel_id=1, source_target_pairs={{1,0},{2,1},{3,2},{5,4},{6,5},{7,6},{9,8},{10,9},{11,10},{13,12},{... | collective-permute-start | bytes 712712 | tf_op jit(solution)/shard_map/ppermute | solution.py:534
  35.1 0.9 collective-permute-done.4.below_ref
  36.0 5.9 %collective-permute-done.5.above_ref = f32[232,256]{1,0:T(8,128)S(1)} collective-permute-done((f32[232,256]{1,0:T(8,128)S(1)}, f32[232,256]{1,0:T(8,128)S(1)}, u32[]{:S(2)}, u32[]{:S(2)}) %collective-permute-start.5) | collective-permute-done | bytes 237600 | tf_op jit(solution)/shard_map/ppermute | solution.py:534
  41.9 7.9 %first_solve.1 = (f32[8,32,256]{2,1,0:T(8,128)S(1)}, f32[4,64,36]{2,1,0:T(8,128)}) custom-call(s32[4]{0:T(128)S(1)} %pad_add_fusion.place_ref, f32[30,40,256]{2,1,0:T(8,128)S(1)} %get-tuple-element.21.sx_ref, f32[232,256]{1,0:T(8,128)S(1)} %collective-permute-done.4.below_ref, f32[232,256]{1,0:T(8,128)S(1)} %collective-permute-done.5.above_ref, ...), custom_call_target="tpu_custom_call" | custom-call | tf_op jit(solution)/shard_map/first_solve/pallas_call | solution.py:244
  49.8 11.0 %all-to-all-start = ((f32[256,1,36]{2,1,0:T(1,128)}), f32[256,1,36]{2,1,0:T(1,128)S(1)}, u32[]{:S(2)}, u32[]{:S(2)}) async-start(f32[256,1,36]{2,1,0:T(1,128)} %bitcast.9), calls=%async_computation | async-start | bytes 262144 | tf_op jit(solution)/shard_map/all_to_all | solution.py:562
  60.9 0.8 dynamic_slice.7
  61.6 11.9 %all-to-all-done = f32[256,1,36]{2,1,0:T(1,128)S(1)} async-done(((f32[256,1,36]{2,1,0:T(1,128)}), f32[256,1,36]{2,1,0:T(1,128)S(1)}, u32[]{:S(2)}, u32[]{:S(2)}) %all-to-all-start) | async-done | bytes 36896 | tf_op jit(solution)/shard_map/all_to_all | solution.py:562
  73.6 2.3 %place_quarter.1 = f32[64,1,384]{2,1,0:T(1,128)} custom-call(s32[4]{0:T(128)S(1)} %pad_add_fusion.place_ref, f32[256,36]{1,0:T(8,128)S(1)} %bitcast.33), custom_call_target="tpu_custom_call" | custom-call | tf_op jit(solution)/shard_map/place_quarter/pallas_call | solution.py:269
  75.8 4.8 %all-to-all-start.1 = ((f32[64,1,384]{2,1,0:T(1,128)}), f32[64,1,384]{2,1,0:T(1,128)S(1)}, u32[]{:S(2)}, u32[]{:S(2)}) async-start(f32[64,1,384]{2,1,0:T(1,128)} %place_quarter.1), calls=%async_computation.1 | async-start | bytes 196608 | tf_op jit(solution)/shard_map/all_to_all | solution.py:564
  80.6 0.7 constant_dynamic-slice_fusion.target_ref
  81.6 8.6 %all-to-all-done.1 = f32[64,1,384]{2,1,0:T(1,128)S(1)} async-done(((f32[64,1,384]{2,1,0:T(1,128)}), f32[64,1,384]{2,1,0:T(1,128)S(1)}, u32[]{:S(2)}, u32[]{:S(2)}) %all-to-all-start.1) | async-done | bytes 98336 | tf_op jit(solution)/shard_map/all_to_all | solution.py:564
  90.2 1.1 copy-done.4
  91.3 42.6 %layer.1 = f32[1,1536]{1,0:T(1,128)S(1)} custom-call(s32[4]{0:T(128)S(1)} %pad_add_fusion.place_ref, bf16[1536,48]{1,0:T(8,128)(2,1)S(1)} %prepare_targets.1.left_ref, bf16[48,24576]{1,0:T(8,128)(2,1)S(1)} %copy-done, f32[8,24576]{1,0:T(8,128)S(1)} %copy-done.4, f32[64,384]{1,0:T(8,128)S(1)} %bitcast.38, f32[1,384]{1,0:T(1,128)S(1)} %broadcast_in_dim.22.fraction_ref), custom_call_target="tpu_custom_call" | custom-call | tf_op jit(solution)/shard_map/layer/pallas_call | solution.py:394
  134.0 8.4 %all-gather = f32[4,1,1536]{2,1,0:T(1,128)S(1)} all-gather(f32[1,1,1536]{2,1,0:T(1,128)S(1)} %bitcast.40), channel_id=1, replica_groups=mesh['brick'=64,'row'=4] {'row'}, dimensions={0}, use_global_device_ids=true | all-gather | bytes 30720 | tf_op jit(solution)/shard_map/all_gather | solution.py:567
  142.4 1.9 %answer.1 = f32[64,384]{1,0:T(8,128)S(1)} custom-call(s32[4]{0:T(128)S(1)} %pad_add_fusion.place_ref, f32[4,1536]{1,0:T(4,128)S(1)} %bitcast.39, f32[256,36]{1,0:T(8,128)S(1)} %bitcast.34), custom_call_target="tpu_custom_call" | custom-call | tf_op jit(solution)/shard_map/answer/pallas_call | solution.py:438
  144.5 13.8 %all_to_all.27 = f32[64,1,384]{2,1,0:T(1,128)S(1)} all-to-all(f32[64,1,384]{2,1,0:T(1,128)S(1)} %copy.25), channel_id=1, replica_groups=mesh['brick'=64,'row'=4] {'brick'}, dimensions={0} | all-to-all | bytes 196608 | tf_op jit(solution)/shard_map/all_to_all | solution.py:569
  158.4 13.0 %second_solve.1 = f32[8,32,256]{2,1,0:T(8,128)} custom-call(s32[4]{0:T(128)S(1)} %pad_add_fusion.place_ref, f32[64,384]{1,0:T(8,128)S(1)} %bitcast.36, f32[8,32,256]{2,1,0:T(8,128)S(1)} %get-tuple-element.25.first_ref), custom_call_target="tpu_custom_call" | custom-call | tf_op jit(solution)/shard_map/second_solve/pallas_call | solution.py:520
  171.3 0.7 copy.26
  (28 shorter events, 1.0 us)
Async XLA Ops:
  0.6 1.1 copy-start.5
  2.1 24.6 %collective-permute-start = (f32[340,256]{1,0:T(8,128)S(1)}, f32[340,256]{1,0:T(8,128)S(1)}, u32[]{:S(2)}, u32[]{:S(2)}) collective-permute-start(f32[340,256]{1,0:T(8,128)S(1)} %get-tuple-element.17), channel_id=1, source_target_pairs={{0,4},{4,8},{8,12},{12,16},{16,20},{20,24},{24,28},{28,32},{32,36}... | collective-permute-start | bytes 1044488 | tf_op jit(solution)/shard_map/ppermute | solution.py:534
  6.5 20.2 %collective-permute-start.1 = (f32[340,256]{1,0:T(8,128)S(1)}, f32[340,256]{1,0:T(8,128)S(1)}, u32[]{:S(2)}, u32[]{:S(2)}) collective-permute-start(f32[340,256]{1,0:T(8,128)S(1)} %get-tuple-element.17), channel_id=1, source_target_pairs={{4,0},{8,4},{12,8},{16,12},{20,16},{24,20},{28,24},{32,28},{36,32}... | collective-permute-start | bytes 1044488 | tf_op jit(solution)/shard_map/ppermute | solution.py:534
  7.8 15.4 %collective-permute-start.2 = (f32[136,256]{1,0:T(8,128)S(1)}, f32[136,256]{1,0:T(8,128)S(1)}, u32[]{:S(2)}, u32[]{:S(2)}) collective-permute-start(f32[136,256]{1,0:T(8,128)S(1)} %get-tuple-element.18), channel_id=1, source_target_pairs={{0,8},{4,12},{8,16},{12,20},{16,24},{20,28},{24,32},{28,36},{32,40... | collective-permute-start | bytes 417800 | tf_op jit(solution)/shard_map/ppermute | solution.py:534
  13.3 13.4 %collective-permute-start.3 = (f32[136,256]{1,0:T(8,128)S(1)}, f32[136,256]{1,0:T(8,128)S(1)}, u32[]{:S(2)}, u32[]{:S(2)}) collective-permute-start(f32[136,256]{1,0:T(8,128)S(1)} %get-tuple-element.19), channel_id=1, source_target_pairs={{8,0},{12,4},{16,8},{20,12},{24,16},{28,20},{32,24},{36,28},{40,32... | collective-permute-start | bytes 417800 | tf_op jit(solution)/shard_map/ppermute | solution.py:534
  17.1 1.4 copy-start.1
  18.5 1.4 copy-start.2
  19.9 15.0 %copy-start.6 = (s32[1,1,64]{2,1,0:T(1,128)S(1)}, s32[1,1,64]{2,1,0:T(1,128)}, u32[]{:S(2)}) copy-start(s32[1,1,64]{2,1,0:T(1,128)} %param.13) | copy-start | bytes 772
  23.2 26.6 %copy-start.3 = (f32[8,24576]{1,0:T(8,128)}, f32[8,24576]{1,0:T(8,128)S(1)}, u32[]{:S(2)}) copy-start(f32[8,24576]{1,0:T(8,128)S(1)} %get-tuple-element.15.moment_ref) | copy-start | bytes 2359300
  27.0 9.1 %collective-permute-start.4 = (f32[232,256]{1,0:T(8,128)S(1)}, f32[232,256]{1,0:T(8,128)S(1)}, u32[]{:S(2)}, u32[]{:S(2)}) collective-permute-start(f32[232,256]{1,0:T(8,128)S(1)} %get-tuple-element.22), channel_id=1, source_target_pairs={{0,1},{1,2},{2,3},{4,5},{5,6},{6,7},{8,9},{9,10},{10,11},{12,13},{... | collective-permute-start | bytes 712712 | tf_op jit(solution)/shard_map/ppermute | solution.py:534
  33.0 8.9 %collective-permute-start.5 = (f32[232,256]{1,0:T(8,128)S(1)}, f32[232,256]{1,0:T(8,128)S(1)}, u32[]{:S(2)}, u32[]{:S(2)}) collective-permute-start(f32[232,256]{1,0:T(8,128)S(1)} %get-tuple-element.23), channel_id=1, source_target_pairs={{1,0},{2,1},{3,2},{5,4},{6,5},{7,6},{9,8},{10,9},{11,10},{13,12},{... | collective-permute-start | bytes 712712 | tf_op jit(solution)/shard_map/ppermute | solution.py:534
  35.1 55.1 %copy-start = (bf16[48,24576]{1,0:T(8,128)(2,1)S(1)}, bf16[48,24576]{1,0:T(8,128)(2,1)}, u32[]{:S(2)}) copy-start(bf16[48,24576]{1,0:T(8,128)(2,1)} %get-tuple-element.14.right_ref) | copy-start | bytes 7077892
  49.8 23.7 %all-to-all-start = ((f32[256,1,36]{2,1,0:T(1,128)}), f32[256,1,36]{2,1,0:T(1,128)S(1)}, u32[]{:S(2)}, u32[]{:S(2)}) async-start(f32[256,1,36]{2,1,0:T(1,128)} %bitcast.9), calls=%async_computation | async-start | bytes 262144 | tf_op jit(solution)/shard_map/all_to_all | solution.py:562
  75.8 14.4 %all-to-all-start.1 = ((f32[64,1,384]{2,1,0:T(1,128)}), f32[64,1,384]{2,1,0:T(1,128)S(1)}, u32[]{:S(2)}, u32[]{:S(2)}) async-start(f32[64,1,384]{2,1,0:T(1,128)} %place_quarter.1), calls=%async_computation.1 | async-start | bytes 196608 | tf_op jit(solution)/shard_map/all_to_all | solution.py:564
  90.2 1.1 copy-start.4
